TPU v7x, 256 devices: a whole 4x4x8 slice. The times are simulated.
256 devices in a mesh: comp: 2 (over core), row: 8 (over z), col: 16 (over y, x).
Axes of the slice: x: 4, y: 4, z: 8, core: 2. Of those that a mesh axis runs over, the one named last changes fastest.
Arguments:
- atmosphere_state: bfloat16 [384, 1024, 512], P('row', 'col', 'comp'), may hold values from -6 to 6
- water_condition: bfloat16 [192, 2048, 256], P('row', 'col', 'comp'), may hold values from -6 to 6
- ocean_cell_mask: int32 [192, 2048], P('row', 'col'), may hold values 0 or 1
- atmos_to_ocean_index: int32 [192, 2048, 4], P('row', 'col'), may hold values from 0 to 3299, as said below
- atmos_to_ocean_weight: float32 [192, 2048, 4], P('row', 'col'), may hold values from 0.1 to 1
- water_source_positions: int32 [384, 1024, 4], P('row', 'col'), may hold values from 0 to 3379, as said below
- water_source_overlay_areas: float32 [384, 1024, 4], P('row', 'col'), may hold values from 0.1 to 1
- flux_weight: bfloat16 [512, 16], P('comp'), may hold values from -0.25 to 0.25
- flux_lift_weight: bfloat16 [16, 256], P(None, 'comp'), may hold values from -1.5 to 1.5
- interface_projection_matrix: bfloat16 [256, 16], P('comp'), may hold values from -0.375 to 0.375
- interface_driving_matrix: bfloat16 [16, 512], P(None, 'comp'), may hold values from -1.5 to 1.5
- forward_basis: bfloat16 [1024, 384, 384], P(('row', 'col')), may hold values from -0.3125 to 0.3125
- inverse_basis: bfloat16 [1024, 384, 384], P(('row', 'col')), may hold values from -0.3125 to 0.3125
- mixing_weight: bfloat16 [512, 512], P(None, 'comp'), may hold values from -0.25 to 0.25
- degree_filter: float32 [384, 512], P(None, 'comp'), may hold values from 0.3 to 3
- first_ocean_kernel: bfloat16 [3, 3, 256, 256], P(None, None, None, 'comp'), may hold values from -0.125 to 0.125
- second_ocean_kernel: bfloat16 [3, 3, 256, 256], P(None, None, None, 'comp'), may hold values from -0.125 to 0.125
Outputs:
- atm_out: bfloat16 [384, 1024, 512], P('row', 'col', 'comp')
- ocean_out: bfloat16 [192, 2048, 256], P('row', 'col', 'comp')
Inputs may be any that keep to these rules, and one draw needn't show every extreme that they name: `atmos_to_ocean_index`: for the ocean cell in row i and column j, each entry names row-major a cell of the block of (50) x (66) cells made of atmosphere block (i // 24, j // 128) and one cycle around it. `water_source_positions`: for the atmosphere cell in row t and column j, each entry names row-major a cell of the block of (26) x (130) cells made of ocean block (t // 48, j // 64) and one cycle around it.
All inputs are finite; a program needn't handle non-finite values. No bound on the sum of `ocean_cell_mask` on one device may be relied on, other than what follows from the above.
Results may differ from a plain program's by a relative error of at most 0.022.
Values may be sent and summed in bfloat16 or wider, within the bound.
A program may use at most 128 MiB of HBM per device.

v0:
```python
import math

import jax
import jax.numpy as jnp
import ml_dtypes
import numpy as np
from jax import lax
from jax.experimental import pallas as pl
from jax.experimental.pallas import tpu as pltpu
from jax.sharding import PartitionSpec as P

BF16 = jnp.bfloat16
F32 = jnp.float32
MESH = pl.DeviceIdType.MESH
LANES = 256


def lon_table(count):
    col_idx = np.arange(count, dtype=np.int64)[:, None]
    coef_idx = np.arange(count, dtype=np.int64)[None, :]
    half_count = count // 2
    freq = np.where(coef_idx <= half_count, coef_idx, coef_idx - half_count)
    phase = (col_idx * freq % count) * (2.0 * math.pi / count)
    values = np.where(coef_idx <= half_count, np.cos(phase), np.sin(phase))
    return (values * math.sqrt(2.0 / count)).astype(ml_dtypes.bfloat16)


def dot(a, b):
    return jnp.dot(a, b, preferred_element_type=F32)


def dot_nt(a, b):
    return lax.dot_general(a, b, (((1,), (1,)), ((), ())), preferred_element_type=F32)


def dot_tn(a, b):
    return lax.dot_general(a, b, (((0,), (0,)), ((), ())), preferred_element_type=F32)


def drain(ref, sem):
    pltpu.make_async_copy(ref, ref, sem).wait()


def gelu(x):
    return jax.nn.gelu(x, approximate=True)


def make_kernel(NR, NC, NX, PT, PM, C, WY, WX, CO, NF, DEG):
    LT = PT // NC
    NLON = NC * PM
    ND = NR * NC
    KB = NLON // ND
    NLAT = NR * PT
    NY = NC // NX
    AR, AC = PT + 2, PM + 2
    OR, OC = WY + 2, WX + 2
    WP = WX + 16
    XR = WY + 4
    HR_ = WY + 2
    FB = NLON // 4

    def kernel(
        atm, water, mask, oidx, ow, aidx, aw, fwt, flw, ipmt, drv, fb_h, ib_h, mw_h, filt_h, k1_h, k2_h,
        tab_h, tabt_h, atm_out, ocean_out,
        atm_v, g1, tabt, tab, sp, rx, rxf, fb, ib, md, mp, mw, filt, qf, qb, vx, bx, gs, hh, lf,
        x, hl, hr, hd, w1, w2, oo, dsc,
        tf, ts, pf, ps, ef, es, efl, efr, esl, esr, rsc, csc, wsc, ss, sr, fx,
        ld, wsend, wrecv, csend, crecv, hsend, hrecv, g1s, g1r, sss, ssr, s2s, r2, mds, mdr,
        q_s, q_r, gss, gsr, hds, hdr, outs, ready,
    ):
        me = lax.axis_index("comp")
        row = lax.axis_index("row")
        col = lax.axis_index("col")
        flat = row * NC + col
        other = 1 - me

        def rmod(v):
            return lax.rem(v + NR, NR)

        def cmod(v):
            return lax.rem(v + NC, NC)

        def shifted(py, px):
            y = lax.rem(col // NX + py, NY)
            xx = lax.rem(lax.rem(col, NX) + px, NX)
            return y * NX + xx

        def send(src, dst, ssem, rsem, dev):
            pltpu.make_async_remote_copy(
                src_ref=src, dst_ref=dst, send_sem=ssem, recv_sem=rsem, device_id=dev, device_id_type=MESH
            ).start()

        def load(i, src, dst):
            pltpu.make_async_copy(src, dst, ld.at[i]).start()

        barrier = pltpu.get_barrier_semaphore()

        def greet(dev):
            pl.semaphore_signal(barrier, inc=1, device_id=dev, device_id_type=MESH)

        for d in range(1, NC):
            greet((me, row, cmod(col + d)))
        for d in range(1, NR):
            greet((me, rmod(row + d), col))
        for dr in (-1, 0, 1):
            for dc in (-1, 0, 1):
                greet((other, rmod(row + dr), cmod(col + dc)))
                if dr and dc:
                    greet((me, rmod(row + dr), cmod(col + dc)))

        load(0, atm, atm_v)
        load(1, water, x.at[me, 2 : 2 + WY, 0:WX])
        load(2, tabt_h, tabt)
        load(3, fb_h, fb)
        load(4, ib_h, ib)
        load(5, mw_h, mw)
        load(6, filt_h, filt)
        load(7, tab_h, tab)
        for a in range(3):
            for b in range(3):
                rows = pl.ds(a * 2 * CO, 2 * CO)
                cols = pl.ds(b * CO, CO)
                pltpu.make_async_copy(k1_h.at[a, b], w1.at[rows, cols], ld.at[8]).start()
                pltpu.make_async_copy(k2_h.at[a, b], w2.at[rows, cols], ld.at[9]).start()

        pl.semaphore_wait(barrier, NC - 1 + NR - 1 + 9 + 4)
        for d in range(1, NR):
            pl.semaphore_signal(ready, inc=1, device_id=(me, rmod(row + d), col), device_id_type=MESH)

        def send_lat(t):
            pltpu.make_async_copy(atm.at[col * LT + t], g1.at[t, pl.ds(col * PM, PM)], g1r.at[t]).start()

            def step(p, _):
                there = shifted(p // NX, lax.rem(p, NX))
                send(
                    atm.at[there * LT + t], g1.at[t, pl.ds(col * PM, PM)], g1s.at[t], g1r.at[t], (me, row, there)
                )
                return 0

            lax.fori_loop(1, NC, step, 0)

        def water_sends(q):
            return [
                (row > 0, water.at[0:2], x.at[me, XR - 2 : XR, 0:WX], (q, rmod(row - 1), col)),
                (row < NR - 1, water.at[WY - 2 : WY], x.at[me, 0:2, 0:WX], (q, rmod(row + 1), col)),
                (col > 0, water.at[:, 0:16], hr.at[me, 2 : 2 + WY], (q, row, cmod(col - 1))),
                (col < NC - 1, water.at[:, WX - 16 : WX], hl.at[me, 2 : 2 + WY], (q, row, cmod(col + 1))),
                ((row > 0) & (col > 0), water.at[0:2, 0:16], hr.at[me, XR - 2 : XR],
                 (q, rmod(row - 1), cmod(col - 1))),
                ((row > 0) & (col < NC - 1), water.at[0:2, WX - 16 : WX], hl.at[me, XR - 2 : XR],
                 (q, rmod(row - 1), cmod(col + 1))),
                ((row < NR - 1) & (col > 0), water.at[WY - 2 : WY, 0:16], hr.at[me, 0:2],
                 (q, rmod(row + 1), cmod(col - 1))),
                ((row < NR - 1) & (col < NC - 1), water.at[WY - 2 : WY, WX - 16 : WX], hl.at[me, 0:2],
                 (q, rmod(row + 1), cmod(col + 1))),
            ]

        def water_recvs(q):
            return [
                (row < NR - 1, x.at[q, XR - 2 : XR, 0:WX]),
                (row > 0, x.at[q, 0:2, 0:WX]),
                (col < NC - 1, hr.at[q, 2 : 2 + WY]),
                (col > 0, hl.at[q, 2 : 2 + WY]),
                ((row < NR - 1) & (col < NC - 1), hr.at[q, XR - 2 : XR]),
                ((row < NR - 1) & (col > 0), hl.at[q, XR - 2 : XR]),
                ((row > 0) & (col < NC - 1), hr.at[q, 0:2]),
                ((row > 0) & (col > 0), hl.at[q, 0:2]),
            ]

        send_lat(0)

        drain(x.at[0, 2 : 2 + WY, 0:WX], ld.at[1])
        wv = x.at[me]

        def project_water(i, _):
            cells = wv[pl.ds(2 + 4 * i, 4), 0:WX, :].reshape(4 * WX, CO)
            got = dot_nt(ipmt[...], cells).astype(BF16)
            for j in range(4):
                ps[me, pl.ds((4 * i + j) * NF, NF), :] = got[:, j * WX : (j + 1) * WX]
            return 0

        lax.fori_loop(0, WY // 4, project_water, 0)
        send(ps.at[me], ps.at[me], csend.at[0], crecv.at[0], (other, row, col))

        drain(atm_v, ld.at[0])

        def project_air(t, _):
            cells = atm_v[pl.ds(t * 4, 4)].reshape(4 * PM, C)
            got = dot_nt(fwt[...], cells)
            zeros = jnp.zeros((NF, 128 - PM), F32)
            for j in range(4):
                part = jnp.concatenate([got[:, j * PM : (j + 1) * PM], zeros], axis=1)
                pf[me, pl.ds((t * 4 + j) * NF, NF), :] = part.astype(BF16)
            return 0

        lax.fori_loop(0, PT // 4, project_air, 0)
        send(pf.at[me], pf.at[me], csend.at[1], crecv.at[1], (other, row, col))

        def both(part):
            return (part[0].astype(F32) + part[1].astype(F32)).astype(BF16)

        lane = lax.broadcasted_iota(jnp.int32, (16, 128), 1)
        line = lax.broadcasted_iota(jnp.int32, (16, 128), 0)

        def pick(cond):
            return jnp.where(cond, 1.0, 0.0).astype(BF16)

        def row_halo(tab_ref, rows, at):
            above = pl.ds((rows + 1) * NF, NF)
            below = pl.ds(rows * NF, NF)

            @pl.when(row > 0)
            def _():
                send(tab_ref.at[0:NF, 0:128], tab_ref.at[below, 0:128], hsend.at[at], hrecv.at[at],
                     (me, rmod(row - 1), col))

            @pl.when(row < NR - 1)
            def _():
                send(tab_ref.at[(rows - 1) * NF : rows * NF, 0:128], tab_ref.at[above, 0:128],
                     hsend.at[at + 1], hrecv.at[at + 1], (me, rmod(row + 1), col))

            @pl.when(row < NR - 1)
            def _():
                drain(tab_ref.at[below, 0:128], hrecv.at[at])

            @pl.when(row == NR - 1)
            def _():
                tab_ref[below, 0:128] = jnp.zeros((NF, 128), BF16)

            @pl.when(row > 0)
            def _():
                drain(tab_ref.at[above, 0:128], hrecv.at[at + 1])

            @pl.when(row == 0)
            def _():
                tab_ref[above, 0:128] = jnp.zeros((NF, 128), BF16)

        def sent(cond, ref, at):
            @pl.when(cond)
            def _():
                drain(ref, hsend.at[at])

        def row_halo_sent(tab_ref, at):
            sent(row > 0, tab_ref.at[0:NF, 0:128], at)
            sent(row < NR - 1, tab_ref.at[0:NF, 0:128], at + 1)

        def col_halo_send(tab_ref, edge, left, right, width, at):
            ends = pick(((line == 0) & (lane == 0)) | ((line == 1) & (lane == width - 1)))
            edge[...] = dot_nt(ends, tab_ref[:, 0:128]).astype(BF16)

            @pl.when(col > 0)
            def _():
                send(edge, right, hsend.at[at], hrecv.at[at], (me, row, cmod(col - 1)))

            @pl.when(col < NC - 1)
            def _():
                send(edge, left, hsend.at[at + 1], hrecv.at[at + 1], (me, row, cmod(col + 1)))

        def col_halo_recv(left, right, at):
            @pl.when(col < NC - 1)
            def _():
                drain(right, hrecv.at[at])

            @pl.when(col == NC - 1)
            def _():
                right[...] = jnp.zeros(right.shape, BF16)

            @pl.when(col > 0)
            def _():
                drain(left, hrecv.at[at + 1])

            @pl.when(col == 0)
            def _():
                left[...] = jnp.zeros(left.shape, BF16)

        def halo_columns(left, right, place):
            from_right = pick((line == 0) & (lane == place))
            from_left = pick((line == 1) & (lane == place + 1))
            return dot_tn(right[...], from_right) + dot_tn(left[...], from_left)

        def regrid(tab_ref, index, weight, rows, cols, block):
            cells = index.astype(F32)
            r_at = jnp.floor((cells + 0.5) * (1.0 / cols))
            c_at = cells - r_at * cols
            rsc[...] = jnp.where(r_at == 0, rows - 1.0, r_at - 1.0)
            csc[...] = jnp.where(c_at == 0, cols - 1.0, c_at - 1.0)
            wsc[...] = weight / jnp.sum(weight, axis=0, keepdims=True)
            width = tab_ref.shape[1]
            at = lax.broadcasted_iota(jnp.int32, (width, LANES), 0).astype(F32)

            def source(k, total):
                r_k = rsc[pl.ds(k, 1), :]
                c_k = csc[pl.ds(k, 1), :]
                w_k = wsc[pl.ds(k, 1), :]
                chosen = jnp.where(at == c_k, 1.0, 0.0).astype(BF16)
                for b in range(rows // block):
                    lines = dot(tab_ref[b * block * NF : (b + 1) * block * NF, :], chosen)
                    for j in range(block):
                        share = jnp.where(r_k == float(b * block + j), w_k, 0.0)
                        total = total + lines[j * NF : (j + 1) * NF] * share
                return total

            return lax.fori_loop(0, 4, source, jnp.zeros((NF, LANES), F32))

        drain(ps.at[0], crecv.at[0])
        ts[0 : WY * NF, 0:128] = both(ps)
        row_halo(ts, WY, 0)
        col_halo_send(ts, es, esl, esr, WX, 4)
        send_lat(1)
        for q in range(2):
            for n, (there, src, dst, dev) in enumerate(water_sends(q)):
                @pl.when(there)
                def _(src=src, dst=dst, dev=dev, n=n, q=q):
                    send(src, dst, wsend.at[n, q], wrecv.at[n, me], dev)
        send(water, x.at[me, 2 : 2 + WY, 0:WX], wsend.at[8, 0], wrecv.at[8, 0], (other, row, col))
        send_lat(2)

        drain(pf.at[0], crecv.at[1])
        tf[0 : PT * NF, :] = both(pf)
        row_halo(tf, PT, 2)
        col_halo_send(tf, ef, efl, efr, PM, 6)

        col_halo_recv(esl, esr, 4)
        row_halo_sent(ts, 0)
        ts[:, 128:256] = halo_columns(esl, esr, 0).astype(BF16)

        def to_air(c, _):
            idx = jnp.concatenate(
                [aidx[c * LT + i] for i in range(LT)] + [jnp.zeros((4, LANES - LT * PM), jnp.int32)], axis=1
            )
            wgt = jnp.concatenate(
                [aw[c * LT + i] for i in range(LT)] + [jnp.ones((4, LANES - LT * PM), F32)], axis=1
            )
            ss[c] = regrid(ts, idx, wgt, OR, OC, 13 if OR % 13 == 0 else 1).astype(BF16)

            @pl.when(c != col)
            def _():
                send(ss.at[c], sr.at[col], sss, ssr, (me, row, c))

            return 0

        lax.fori_loop(0, NC, to_air, 0)
        pltpu.make_async_copy(ss.at[col], sr.at[col], ssr).start()

        def lift_here(c, _):
            term = dot_tn(ss[c], drv[...])
            for i in range(LT):
                t = c * LT + i
                lf[t] = (atm_v[t].astype(F32) + term[i * PM : (i + 1) * PM]).astype(BF16)
            return 0

        lax.fori_loop(0, NC, lift_here, 0)

        drain(sr, ssr)

        def lift_terms(c, _):
            dsc[c] = dot_tn(sr[c], drv[...])
            return 0

        lax.fori_loop(0, NC, lift_terms, 0)

        drain(tabt, ld.at[2])
        pl.semaphore_wait(ready, NR - 1)

        for t in range(LT):
            drain(g1.at[t], g1r.at[t])

            def lift_lat(c, _, t=t):
                rows = pl.ds(pl.multiple_of(c * PM, PM), PM)
                g1[t, rows, :] = (
                    g1[t, rows, :].astype(F32) + dsc[c, t * PM : (t + 1) * PM, :]
                ).astype(BF16)
                return 0

            lax.fori_loop(0, NC, lift_lat, 0)

            def analyse(b, _, t=t):
                rows = pl.ds(pl.multiple_of(b * FB, FB), FB)
                got = dot(tabt[rows, :], g1[t])
                halves = [got[:, h * 128 : (h + 1) * 128].reshape(FB // 8, 8, 128) for h in range(2)]
                sp[t, pl.ds(b * (FB // 8), FB // 8)] = jnp.concatenate(halves, axis=1).astype(BF16)
                return 0

            lax.fori_loop(0, 4, analyse, 0)
            pltpu.make_async_copy(sp.at[t, flat], rx.at[flat * LT + t], r2.at[t]).start()

            def scatter(p, _, t=t):
                r_to = rmod(row + p // NC)
                c_to = shifted(lax.rem(p, NC) // NX, lax.rem(p, NX))
                send(sp.at[t, r_to * NC + c_to], rx.at[flat * LT + t], s2s.at[t], r2.at[t], (me, r_to, c_to))
                return 0

            lax.fori_loop(1, ND, scatter, 0)

        for q in range(2):
            for n, (there, dst) in enumerate(water_recvs(q)):
                @pl.when(there)
                def _(dst=dst, n=n, q=q):
                    drain(dst, wrecv.at[n, q])
        drain(x.at[0, 2 : 2 + WY, 0:WX], wrecv.at[8, 0])

        @pl.when(row == 0)
        def _():
            x[:, 0:2, 0:WX, :] = jnp.zeros((2, 2, WX, CO), BF16)

        @pl.when(row == NR - 1)
        def _():
            x[:, XR - 2 : XR, 0:WX, :] = jnp.zeros((2, 2, WX, CO), BF16)

        def side(i, _):
            inside = ((i >= 2) | (row > 0)) & ((i < XR - 2) | (row < NR - 1))
            sub = lax.broadcasted_iota(jnp.int32, (16, CO), 0)
            for q in range(2):
                from_right = jnp.where((sub < 2) & inside & (col < NC - 1), hr[q, i].astype(F32), 0.0)
                from_left = jnp.where((sub >= 14) & inside & (col > 0), hl[q, i].astype(F32), 0.0)
                x[q, i, WX:WP, :] = (from_right + from_left).astype(BF16)
            return 0

        lax.fori_loop(0, XR, side, 0)
        drain(w1, ld.at[8])

        def taps(src, weight, first, count):
            lhs = jnp.concatenate(
                [
                    jnp.concatenate([src[q, first + j + a] for a in range(3) for q in range(2)], axis=1)
                    for j in range(count)
                ],
                axis=0,
            )
            got = dot(lhs, weight[...])
            outs_ = []
            for j in range(count):
                part = got[j * WP : (j + 1) * WP]
                outs_.append(
                    pltpu.roll(part[:, 0:CO], 1, 0)
                    + part[:, CO : 2 * CO]
                    + pltpu.roll(part[:, 2 * CO : 3 * CO], WP - 1, 0)
                )
            return outs_

        def conv_first(i, _):
            place = lax.broadcasted_iota(jnp.int32, (WP, CO), 0)
            edge = ((place == WP - 1) & (col == 0)) | ((place == WX) & (col == NC - 1))
            for j, out in enumerate(taps(x, w1, 2 * i, 2)):
                h = 2 * i + j
                outside = ((h == 0) & (row == 0)) | ((h == HR_ - 1) & (row == NR - 1))
                hd[me, h] = jnp.where(edge | outside, 0.0, gelu(out)).astype(BF16)
            return 0

        lax.fori_loop(0, HR_ // 2, conv_first, 0)
        send(hd.at[me], hd.at[me], hds, hdr, (other, row, col))

        col_halo_recv(efl, efr, 6)
        row_halo_sent(tf, 2)
        tf[...] = (tf[...].astype(F32) + halo_columns(efl, efr, PM)).astype(BF16)

        def to_ocean(i, _):
            idx = jnp.concatenate([oidx[2 * i], oidx[2 * i + 1]], axis=1)
            wgt = jnp.concatenate([ow[2 * i], ow[2 * i + 1]], axis=1)
            fx[i] = regrid(tf, idx, wgt, AR, AC, 10 if AR % 10 == 0 else 1).astype(BF16)
            return 0

        lax.fori_loop(0, WY // 2, to_ocean, 0)

        drain(hd.at[0], hdr)
        drain(w2, ld.at[9])

        def conv_second(i, _):
            outs_ = taps(hd, w2, 2 * i, 2)
            sixteenth = jnp.full((NF, CO), 1.0 / NF, BF16)
            for j in range(2):
                r = 2 * i + j
                lift = dot_tn(fx[i, :, j * WX : (j + 1) * WX], flw[...])
                line_mask = jnp.broadcast_to(mask[pl.ds(r, 1), :].astype(F32), (NF, WX)).astype(BF16)
                keep = dot_tn(line_mask, sixteenth)
                here = x[me, r + 2, 0:WX, :].astype(F32)
                oo[r] = (here + keep * (outs_[j][0:WX] + lift)).astype(BF16)
            return 0

        lax.fori_loop(0, WY // 2, conv_second, 0)
        pltpu.make_async_copy(oo, ocean_out, outs.at[0]).start()

        drain(fb, ld.at[3])
        for t in range(LT):
            drain(rx.at[0:ND], r2.at[t])
        TB = 32 if NLAT % 32 == 0 else 8

        def widen(i, _):
            rows = pl.ds(pl.multiple_of(i * TB, TB), TB)
            out_rows = pl.ds(pl.multiple_of(i * TB * 16, TB * 16), TB * 16)
            rxf[out_rows, :] = rx[rows].astype(F32).reshape(TB * 16, 128)
            return 0

        lax.fori_loop(0, NLAT // TB, widen, 0)

        def to_modes(k, _):
            col_k = jnp.concatenate(
                [rxf[pl.ds(k + 8 * h, NLAT, stride=16), :] for h in range(2)], axis=1
            ).astype(BF16)
            md[k] = dot(fb[k], col_k).astype(BF16)
            send(md.at[k], mp.at[k], mds.at[k], mdr.at[k], (other, row, col))
            return 0

        lax.fori_loop(0, KB, to_modes, 0)
        drain(ib, ld.at[4])
        drain(mw, ld.at[5])
        drain(filt, ld.at[6])

        def to_synth(k, _):
            drain(mp.at[k], mdr.at[k])
            mixed = dot(md[k], mw[pl.ds(pl.multiple_of(me * C, C), C), :])
            mixed = mixed + dot(mp[k], mw[pl.ds(pl.multiple_of(other * C, C), C), :])
            mixed = (mixed * filt[...]).astype(BF16)
            got = dot(ib[k], mixed)
            for h in range(2):
                qf[pl.ds(k + 8 * h, NLAT, stride=16), :] = got[:, h * 128 : (h + 1) * 128]
            return 0

        lax.fori_loop(0, KB, to_synth, 0)

        def narrow(i, _):
            rows = pl.ds(pl.multiple_of(i * TB, TB), TB)
            in_rows = pl.ds(pl.multiple_of(i * TB * 16, TB * 16), TB * 16)
            qb[rows] = qf[in_rows, :].reshape(TB, 16, 128).astype(BF16)
            return 0

        lax.fori_loop(0, NLAT // TB, narrow, 0)

        for t in range(LT):
            pltpu.make_async_copy(qb.at[flat * LT + t], vx.at[t, flat], q_r.at[t]).start()

            def gather_back(p, _, t=t):
                r_to = rmod(row + p // NC)
                c_to = shifted(lax.rem(p, NC) // NX, lax.rem(p, NX))
                send(
                    qb.at[(r_to * NC + c_to) * LT + t], vx.at[t, flat], q_s.at[t], q_r.at[t], (me, r_to, c_to)
                )
                return 0

            lax.fori_loop(1, ND, gather_back, 0)

        drain(tab, ld.at[7])
        for t in range(LT):
            drain(vx.at[t], q_r.at[t])
            for h in range(2):
                part = vx[t].astype(F32)[:, 8 * h : 8 * h + 8, :].reshape(NLON, 128)
                bx[:, h * 128 : (h + 1) * 128] = part.astype(BF16)

            def synthesise(b, _, t=t):
                rows = pl.ds(pl.multiple_of(b * FB, FB), FB)
                gs[t, rows, :] = dot(tab[rows, :], bx[...]).astype(BF16)
                return 0

            lax.fori_loop(0, 4, synthesise, 0)
            pltpu.make_async_copy(
                gs.at[t, pl.ds(col * PM, PM)], hh.at[col * LT + t], gsr.at[t]
            ).start()

            def home(p, _, t=t):
                there = shifted(p // NX, lax.rem(p, NX))
                send(
                    gs.at[t, pl.ds(there * PM, PM)], hh.at[col * LT + t], gss.at[t], gsr.at[t], (me, row, there)
                )
                return 0

            lax.fori_loop(1, NC, home, 0)

        for t in range(LT):
            drain(hh.at[0:NC], gsr.at[t])

            def finish(c, _, t=t):
                i = c * LT + t
                lf[i] = (lf[i].astype(F32) + gelu(hh[i].astype(F32))).astype(BF16)
                return 0

            lax.fori_loop(0, NC, finish, 0)
        pltpu.make_async_copy(lf, atm_out, outs.at[1]).start()

        for t in range(LT):
            drain(g1.at[t, 0 : (NC - 1) * PM], g1s.at[t])
            drain(sp.at[t, 0 : ND - 1], s2s.at[t])
            drain(vx.at[t, 0 : ND - 1], q_s.at[t])
            drain(gs.at[t, 0 : (NC - 1) * PM], gss.at[t])
        drain(sr.at[0 : NC - 1], sss)
        for q in range(2):
            for n, (there, src, dst, dev) in enumerate(water_sends(q)):
                @pl.when(there)
                def _(src=src, n=n, q=q):
                    drain(src, wsend.at[n, q])
        drain(water, wsend.at[8, 0])
        drain(ps.at[0], csend.at[0])
        drain(pf.at[0], csend.at[1])
        drain(hd.at[0], hds)
        for k in range(KB):
            drain(mp.at[k], mds.at[k])
        for at, edge in ((4, es), (6, ef)):
            sent(col > 0, edge, at)
            sent(col < NC - 1, edge, at + 1)
        drain(oo, outs.at[0])
        drain(lf, outs.at[1])

    v = pltpu.VMEM
    dma = pltpu.SemaphoreType.DMA
    scratch = [
        v((PT, PM, C), BF16), v((LT, NLON, C), BF16), v((NLON, NLON), BF16), v((NLON, NLON), BF16),
        v((LT, ND, 16, 128), BF16), v((NLAT, 16, 128), BF16), v((NLAT * 16, 128), F32),
        v((KB, DEG, NLAT), BF16), v((KB, NLAT, DEG), BF16), v((KB, DEG, C), BF16), v((KB, DEG, C), BF16),
        v((2 * C, C), BF16), v((DEG, C), F32), v((NLAT * 16, 128), F32), v((NLAT, 16, 128), BF16),
        v((LT, ND, 16, 128), BF16), v((NLON, C), BF16), v((LT, NLON, C), BF16), v((PT, PM, C), BF16),
        v((PT, PM, C), BF16),
        v((2, XR, WP, CO), BF16), v((2, XR, 16, CO), BF16), v((2, XR, 16, CO), BF16), v((2, HR_, WP, CO), BF16),
        v((6 * CO, 3 * CO), BF16), v((6 * CO, 3 * CO), BF16), v((WY, WX, CO), BF16),
        v((NC, LANES, C), F32),
        v((AR * NF, 128), BF16), v((OR * NF, 256), BF16), v((2, PT * NF, 128), BF16), v((2, WY * NF, 128), BF16),
        v((16, AR * NF), BF16), v((16, OR * NF), BF16),
        v((16, AR * NF), BF16), v((16, AR * NF), BF16), v((16, OR * NF), BF16), v((16, OR * NF), BF16),
        v((4, LANES), F32), v((4, LANES), F32), v((4, LANES), F32),
        v((NC, NF, LANES), BF16), v((NC, NF, LANES), BF16), v((WY // 2, NF, LANES), BF16),
        dma((10,)), dma((9, 2)), dma((9, 2)), dma((2,)), dma((2,)), dma((8,)), dma((8,)),
        dma((LT,)), dma((LT,)), dma, dma, dma((LT,)), dma((LT,)), dma((KB,)), dma((KB,)),
        dma((LT,)), dma((LT,)), dma((LT,)), dma((LT,)), dma, dma, dma((2,)), pltpu.SemaphoreType.REGULAR,
    ]
    any_ = pl.BlockSpec(memory_space=pl.ANY)
    vm = pl.BlockSpec(memory_space=pltpu.VMEM)
    return pl.pallas_call(
        kernel,
        out_shape=(
            jax.ShapeDtypeStruct((PT, PM, C), BF16),
            jax.ShapeDtypeStruct((WY, WX, CO), BF16),
        ),
        in_specs=[any_, any_] + [vm] * 9 + [any_] * 8,
        out_specs=(any_, any_),
        scratch_shapes=scratch,
        compiler_params=pltpu.CompilerParams(
            collective_id=0, has_side_effects=True, vmem_limit_bytes=60 * 1024 * 1024
        ),
        cost_estimate=pl.CostEstimate(flops=9_000_000_000, bytes_accessed=20_000_000, transcendentals=2_000_000),
        name="coupled_step",
    )


def solution(mesh):
    NR, NC = mesh.shape["row"], mesh.shape["col"]
    NX = 4 if NC == 16 else NC

    def local(
        atmosphere_state, water_condition, ocean_cell_mask, atmos_to_ocean_index, atmos_to_ocean_weight,
        water_source_positions, water_source_overlay_areas, flux_weight, flux_lift_weight,
        interface_projection_matrix, interface_driving_matrix, forward_basis, inverse_basis,
        mixing_weight, degree_filter, first_ocean_kernel, second_ocean_kernel,
    ):
        PT, PM, C = atmosphere_state.shape
        WY, WX, CO = water_condition.shape
        table = lon_table(NC * PM)
        step = make_kernel(
            NR, NC, NX, PT, PM, C, WY, WX, CO, flux_weight.shape[1], forward_basis.shape[1]
        )
        return step(
            atmosphere_state,
            water_condition,
            ocean_cell_mask,
            jnp.swapaxes(atmos_to_ocean_index, 1, 2),
            jnp.swapaxes(atmos_to_ocean_weight, 1, 2),
            jnp.swapaxes(water_source_positions, 1, 2),
            jnp.swapaxes(water_source_overlay_areas, 1, 2),
            flux_weight.T,
            flux_lift_weight,
            interface_projection_matrix.T,
            interface_driving_matrix,
            forward_basis,
            inverse_basis,
            mixing_weight,
            degree_filter,
            first_ocean_kernel,
            second_ocean_kernel,
            jnp.asarray(table),
            jnp.asarray(np.ascontiguousarray(table.T)),
        )

    placed = (
        P("row", "col", "comp"),
        P("row", "col", "comp"),
        P("row", "col"),
        P("row", "col", None),
        P("row", "col", None),
        P("row", "col", None),
        P("row", "col", None),
        P("comp", None),
        P(None, "comp"),
        P("comp", None),
        P(None, "comp"),
        P(("row", "col"), None, None),
        P(("row", "col"), None, None),
        P(None, "comp"),
        P(None, "comp"),
        P(None, None, None, "comp"),
        P(None, None, None, "comp"),
    )
    return jax.shard_map(
        local,
        mesh=mesh,
        in_specs=placed,
        out_specs=(P("row", "col", "comp"), P("row", "col", "comp")),
        check_vma=False,
    )
```

profile of v0, /device:TPU:8, one launch (start us, length us, event | category | flops | bytes accessed | tf_op | source)
XLA Modules:
  0.0 151.5 jit_solution(15123185970598091420)
XLA Ops:
  0.6 147.2 %coupled_step.1 = (bf16[48,64,256]{2,1,0:T(8,128)(2,1)}, bf16[24,128,128]{2,1,0:T(8,128)(2,1)}) custom-call(bf16[48,64,256]{2,1,0:T(8,128)(2,1)} %atm.1, bf16[24,128,128]{2,1,0:T(8,128)(2,1)} %water.1, s32[24,128]{1,0:T(8,128)} %mask.1, s32[24,4,128]{2,1,0:T(4,128)} %bitcast.8, f32[24,4,128]{2,1,0:T(4,128)} %bitcast.9, s32[48,4,64]{2,1,0:T(4,128)} %bitcast.6, ...), custom_call_target="tpu_custom_call" | custom-call | flops 8999999488 | bytes 20000000 | tf_op jit(solution)/shard_map/coupled_step/pallas_call | solution.py:658
  147.8 0.0 copy-start
  147.8 2.8 %copy.23 = bf16[48,64,256]{2,1,0:T(8,128)(2,1)} copy(bf16[48,64,256]{2,1,0:T(8,128)(2,1)} %get-tuple-element.4) | data formatting | bytes 3145728
  150.6 0.0 copy-done
  150.7 0.9 copy.24
Async XLA Ops:
  147.8 2.8 %copy-start = (bf16[24,128,128]{2,1,0:T(8,128)(2,1)S(1)}, bf16[24,128,128]{2,1,0:T(8,128)(2,1)}, u32[]{:S(2)}) copy-start(bf16[24,128,128]{2,1,0:T(8,128)(2,1)} %get-tuple-element.5) | copy-start | bytes 2359300
where the time goes:
time: 153 us; the launch traced here: 152 us
  Pallas kernels  147 us (96%)
  local copies, waits for them, and re-layouts  3.68 us (2%)
    pallas_call x1, Pallas kernels, local(): step(atmosphere_state, water_condition, ocean_cell_mask, jnp.swapaxes(atm...  147 us
    unnamed x4, local copies, waits for them, and re-layouts  3.68 us

commit v1 on v0

--- a/solution.py
+++ b/solution.py
@@ -52,6 +52,7 @@
     KB = NLON // ND
     NLAT = NR * PT
     NY = NC // NX
+    HC, HO = NC // 2, WY // 4
     AR, AC = PT + 2, PM + 2
     OR, OC = WY + 2, WX + 2
     WP = WX + 16
@@ -60,13 +61,14 @@
     FB = NLON // 4
 
     def kernel(
-        atm, water, mask, oidx, ow, aidx, aw, fwt, flw, ipmt, drv, fb_h, ib_h, mw_h, filt_h, k1_h, k2_h,
-        tab_h, tabt_h, atm_out, ocean_out,
-        atm_v, g1, tabt, tab, sp, rx, rxf, fb, ib, md, mp, mw, filt, qf, qb, vx, bx, gs, hh, lf,
+        atm, water, mask_h, oidx_h, ow_h, aidx_h, aw_h, fwt_h, flw_h, ipmt_h, drv_h, fb_h, ib_h, mw_h, filt_h,
+        k1_h, k2_h, tab_h, tabt_h, lifted_out, grid_out, ocean_out,
+        mask, oidx, ow, aidx, aw, fwt, flw, ipmt, drv,
+        atm_v, g1, tabt, tab, sp, rx, rxf, fb, ib, md, mp, mw, filt, qf, qb, vx, bx, gs, lf, fbp, acc, ms,
         x, hl, hr, hd, w1, w2, oo, dsc,
         tf, ts, pf, ps, ef, es, efl, efr, esl, esr, rsc, csc, wsc, ss, sr, fx,
         ld, wsend, wrecv, csend, crecv, hsend, hrecv, g1s, g1r, sss, ssr, s2s, r2, mds, mdr,
-        q_s, q_r, gss, gsr, hds, hdr, outs, ready,
+        q_s, q_r, gss, gsr, hds, hdr, outs, shs, shr, fxs, fxr, ready,
     ):
         me = lax.axis_index("comp")
         row = lax.axis_index("row")
@@ -84,6 +86,9 @@
             y = lax.rem(col // NX + py, NY)
             xx = lax.rem(lax.rem(col, NX) + px, NX)
             return y * NX + xx
+
+        def partner(p):
+            return rmod(row + lax.rem(p, NR)), shifted(p // (NR * NX), lax.rem(p // NR, NX))
 
         def send(src, dst, ssem, rsem, dev):
             pltpu.make_async_remote_copy(
@@ -108,32 +113,52 @@
                 if dr and dc:
                     greet((me, rmod(row + dr), cmod(col + dc)))
 
+        load(1, water, x.at[me, 2 : 2 + WY, 0:WX])
+        load(10, ipmt_h, ipmt)
         load(0, atm, atm_v)
-        load(1, water, x.at[me, 2 : 2 + WY, 0:WX])
+        for n, (src, dst) in enumerate(
+            ((fwt_h, fwt), (aidx_h, aidx), (aw_h, aw), (drv_h, drv), (mask_h, mask), (oidx_h, oidx), (ow_h, ow),
+             (flw_h, flw))
+        ):
+            load(11 + n, src, dst)
         load(2, tabt_h, tabt)
         load(3, fb_h, fb)
-        load(4, ib_h, ib)
-        load(5, mw_h, mw)
-        load(6, filt_h, filt)
-        load(7, tab_h, tab)
         for a in range(3):
             for b in range(3):
                 rows = pl.ds(a * 2 * CO, 2 * CO)
                 cols = pl.ds(b * CO, CO)
                 pltpu.make_async_copy(k1_h.at[a, b], w1.at[rows, cols], ld.at[8]).start()
                 pltpu.make_async_copy(k2_h.at[a, b], w2.at[rows, cols], ld.at[9]).start()
-
+        load(5, mw_h, mw)
+        load(6, filt_h, filt)
+        load(4, ib_h, ib)
+        load(7, tab_h, tab)
+
+        drain(x.at[0, 2 : 2 + WY, 0:WX], ld.at[1])
+        drain(ipmt, ld.at[10])
+        wv = x.at[me]
+
+        def project_water(i, _):
+            cells = wv[pl.ds(2 + 4 * i, 4), 0:WX, :].reshape(4 * WX, CO)
+            got = dot_nt(ipmt[...], cells).astype(BF16)
+            for j in range(4):
+                ps[me, pl.ds((4 * i + j) * NF, NF), :] = got[:, j * WX : (j + 1) * WX]
+            return 0
+
+        lax.fori_loop(0, WY // 4, project_water, 0)
         pl.semaphore_wait(barrier, NC - 1 + NR - 1 + 9 + 4)
         for d in range(1, NR):
             pl.semaphore_signal(ready, inc=1, device_id=(me, rmod(row + d), col), device_id_type=MESH)
 
+        send(ps.at[me], ps.at[me], csend.at[0], crecv.at[0], (other, row, col))
+
         def send_lat(t):
-            pltpu.make_async_copy(atm.at[col * LT + t], g1.at[t, pl.ds(col * PM, PM)], g1r.at[t]).start()
+            pltpu.make_async_copy(atm.at[t * NC + col], g1.at[t, pl.ds(col * PM, PM)], g1r.at[t]).start()
 
             def step(p, _):
                 there = shifted(p // NX, lax.rem(p, NX))
                 send(
-                    atm.at[there * LT + t], g1.at[t, pl.ds(col * PM, PM)], g1s.at[t], g1r.at[t], (me, row, there)
+                    atm.at[t * NC + there], g1.at[t, pl.ds(col * PM, PM)], g1s.at[t], g1r.at[t], (me, row, there)
                 )
                 return 0
 
@@ -169,20 +194,16 @@
 
         send_lat(0)
 
-        drain(x.at[0, 2 : 2 + WY, 0:WX], ld.at[1])
-        wv = x.at[me]
-
-        def project_water(i, _):
-            cells = wv[pl.ds(2 + 4 * i, 4), 0:WX, :].reshape(4 * WX, CO)
-            got = dot_nt(ipmt[...], cells).astype(BF16)
-            for j in range(4):
-                ps[me, pl.ds((4 * i + j) * NF, NF), :] = got[:, j * WX : (j + 1) * WX]
-            return 0
-
-        lax.fori_loop(0, WY // 4, project_water, 0)
-        send(ps.at[me], ps.at[me], csend.at[0], crecv.at[0], (other, row, col))
-
+        def water_send(first, last):
+            for q in range(2):
+                for n, (there, src, dst, dev) in enumerate(water_sends(q)[first:last]):
+                    @pl.when(there)
+                    def _(src=src, dst=dst, dev=dev, n=n, q=q):
+                        send(src, dst, wsend.at[first + n, q], wrecv.at[first + n, me], dev)
+
+        water_send(0, 2)
         drain(atm_v, ld.at[0])
+        drain(fwt, ld.at[11])
 
         def project_air(t, _):
             cells = atm_v[pl.ds(t * 4, 4)].reshape(4 * PM, C)
@@ -205,7 +226,7 @@
         def pick(cond):
             return jnp.where(cond, 1.0, 0.0).astype(BF16)
 
-        def row_halo(tab_ref, rows, at):
+        def row_halo_send(tab_ref, rows, at):
             above = pl.ds((rows + 1) * NF, NF)
             below = pl.ds(rows * NF, NF)
 
@@ -218,6 +239,10 @@
             def _():
                 send(tab_ref.at[(rows - 1) * NF : rows * NF, 0:128], tab_ref.at[above, 0:128],
                      hsend.at[at + 1], hrecv.at[at + 1], (me, rmod(row + 1), col))
+
+        def row_halo_recv(tab_ref, rows, at):
+            above = pl.ds((rows + 1) * NF, NF)
+            below = pl.ds(rows * NF, NF)
 
             @pl.when(row < NR - 1)
             def _():
@@ -304,53 +329,50 @@
 
         drain(ps.at[0], crecv.at[0])
         ts[0 : WY * NF, 0:128] = both(ps)
-        row_halo(ts, WY, 0)
+        row_halo_send(ts, WY, 0)
+        row_halo_recv(ts, WY, 0)
         col_halo_send(ts, es, esl, esr, WX, 4)
         send_lat(1)
-        for q in range(2):
-            for n, (there, src, dst, dev) in enumerate(water_sends(q)):
-                @pl.when(there)
-                def _(src=src, dst=dst, dev=dev, n=n, q=q):
-                    send(src, dst, wsend.at[n, q], wrecv.at[n, me], dev)
         send(water, x.at[me, 2 : 2 + WY, 0:WX], wsend.at[8, 0], wrecv.at[8, 0], (other, row, col))
-        send_lat(2)
 
         drain(pf.at[0], crecv.at[1])
         tf[0 : PT * NF, :] = both(pf)
-        row_halo(tf, PT, 2)
-        col_halo_send(tf, ef, efl, efr, PM, 6)
+        row_halo_send(tf, PT, 2)
 
         col_halo_recv(esl, esr, 4)
         row_halo_sent(ts, 0)
         ts[:, 128:256] = halo_columns(esl, esr, 0).astype(BF16)
 
-        def to_air(c, _):
+        for n, ref in ((12, aidx), (13, aw), (14, drv)):
+            drain(ref, ld.at[n])
+
+        def to_air(i, _):
+            c = me * HC + i
             idx = jnp.concatenate(
-                [aidx[c * LT + i] for i in range(LT)] + [jnp.zeros((4, LANES - LT * PM), jnp.int32)], axis=1
+                [aidx[t * NC + c] for t in range(LT)] + [jnp.zeros((4, LANES - LT * PM), jnp.int32)], axis=1
             )
             wgt = jnp.concatenate(
-                [aw[c * LT + i] for i in range(LT)] + [jnp.ones((4, LANES - LT * PM), F32)], axis=1
+                [aw[t * NC + c] for t in range(LT)] + [jnp.ones((4, LANES - LT * PM), F32)], axis=1
             )
             ss[c] = regrid(ts, idx, wgt, OR, OC, 13 if OR % 13 == 0 else 1).astype(BF16)
+            send(ss.at[c], sr.at[col], sss, ssr, (other, row, c))
+            send(ss.at[c], ss.at[c], shs, shr, (other, row, col))
 
             @pl.when(c != col)
             def _():
                 send(ss.at[c], sr.at[col], sss, ssr, (me, row, c))
 
-            return 0
-
-        lax.fori_loop(0, NC, to_air, 0)
-        pltpu.make_async_copy(ss.at[col], sr.at[col], ssr).start()
-
-        def lift_here(c, _):
-            term = dot_tn(ss[c], drv[...])
-            for i in range(LT):
-                t = c * LT + i
-                lf[t] = (atm_v[t].astype(F32) + term[i * PM : (i + 1) * PM]).astype(BF16)
-            return 0
-
-        lax.fori_loop(0, NC, lift_here, 0)
-
+            @pl.when(c == col)
+            def _():
+                pltpu.make_async_copy(ss.at[c], sr.at[col], ssr).start()
+
+            return 0
+
+        lax.fori_loop(0, HC, to_air, 0)
+        send_lat(2)
+        water_send(2, 8)
+
+        drain(tabt, ld.at[2])
         drain(sr, ssr)
 
         def lift_terms(c, _):
@@ -359,7 +381,6 @@
 
         lax.fori_loop(0, NC, lift_terms, 0)
 
-        drain(tabt, ld.at[2])
         pl.semaphore_wait(ready, NR - 1)
 
         for t in range(LT):
@@ -382,15 +403,41 @@
                 return 0
 
             lax.fori_loop(0, 4, analyse, 0)
-            pltpu.make_async_copy(sp.at[t, flat], rx.at[flat * LT + t], r2.at[t]).start()
+            pltpu.make_async_copy(sp.at[t, flat], rx.at[t, flat], r2.at[t]).start()
 
             def scatter(p, _, t=t):
-                r_to = rmod(row + p // NC)
-                c_to = shifted(lax.rem(p, NC) // NX, lax.rem(p, NX))
-                send(sp.at[t, r_to * NC + c_to], rx.at[flat * LT + t], s2s.at[t], r2.at[t], (me, r_to, c_to))
+                r_to, c_to = partner(p)
+                send(sp.at[t, r_to * NC + c_to], rx.at[t, flat], s2s.at[t], r2.at[t], (me, r_to, c_to))
                 return 0
 
             lax.fori_loop(1, ND, scatter, 0)
+
+        drain(ss.at[0:HC], shr)
+
+        def lift_here(c, _):
+            term = dot_tn(ss[c], drv[...])
+            for t in range(LT):
+                n = t * NC + c
+                lf[n] = (atm_v[n].astype(F32) + term[t * PM : (t + 1) * PM]).astype(BF16)
+            return 0
+
+        lax.fori_loop(0, NC, lift_here, 0)
+        pltpu.make_async_copy(lf, lifted_out, outs.at[1]).start()
+
+        drain(fb, ld.at[3])
+        lat_in = lax.broadcasted_iota(jnp.int32, (NLAT, NLAT), 0)
+        lat_to = lax.broadcasted_iota(jnp.int32, (NLAT, NLAT), 1)
+        t_to, d_to = lat_to // ND, lax.rem(lat_to, ND)
+        order = pick(lat_in == (d_to // NC) * PT + t_to * NC + lax.rem(d_to, NC))
+
+        def reorder(k, _):
+            fbp[k] = dot(fb[k], order).astype(BF16)
+            return 0
+
+        lax.fori_loop(0, KB, reorder, 0)
+
+        row_halo_recv(tf, PT, 2)
+        col_halo_send(tf, ef, efl, efr, PM, 6)
 
         for q in range(2):
             for n, (there, dst) in enumerate(water_recvs(q)):
@@ -454,15 +501,101 @@
         row_halo_sent(tf, 2)
         tf[...] = (tf[...].astype(F32) + halo_columns(efl, efr, PM)).astype(BF16)
 
-        def to_ocean(i, _):
+        for n, ref in ((15, mask), (16, oidx), (17, ow), (18, flw)):
+            drain(ref, ld.at[n])
+
+        def to_ocean(j, _):
+            i = me * HO + j
             idx = jnp.concatenate([oidx[2 * i], oidx[2 * i + 1]], axis=1)
             wgt = jnp.concatenate([ow[2 * i], ow[2 * i + 1]], axis=1)
             fx[i] = regrid(tf, idx, wgt, AR, AC, 10 if AR % 10 == 0 else 1).astype(BF16)
-            return 0
-
-        lax.fori_loop(0, WY // 2, to_ocean, 0)
+            send(fx.at[i], fx.at[i], fxs, fxr, (other, row, col))
+            return 0
+
+        lax.fori_loop(0, HO, to_ocean, 0)
+
+        TB = 32 if ND % 32 == 0 else 8
+
+        def widen(t):
+            drain(rx.at[t], r2.at[t])
+
+            def step(i, _):
+                rows = pl.ds(pl.multiple_of(i * TB, TB), TB)
+                out_rows = pl.ds(pl.multiple_of((t * ND + i * TB) * 16, TB * 16), TB * 16)
+                rxf[out_rows, :] = rx[t, rows].astype(F32).reshape(TB * 16, 128)
+                return 0
+
+            lax.fori_loop(0, ND // TB, step, 0)
+
+        def spectra_of(k, first, last):
+            count = (last - first) * ND
+            return jnp.concatenate(
+                [rxf[pl.ds(first * ND * 16 + k + 8 * h, count, stride=16), :] for h in range(2)], axis=1
+            ).astype(BF16)
+
+        for t in range(LT - 1):
+            widen(t)
+        SPLIT = (LT - 1) * ND
+
+        def to_modes_first(k, _):
+            acc[k] = dot(fbp[k, :, 0:SPLIT], spectra_of(k, 0, LT - 1))
+            return 0
+
+        lax.fori_loop(0, KB, to_modes_first, 0)
+        drain(mw, ld.at[5])
+        drain(filt, ld.at[6])
+        drain(ib, ld.at[4])
+        widen(LT - 1)
+
+        def to_modes(k, _):
+            md[k] = (acc[k] + dot(fbp[k, :, SPLIT:NLAT], spectra_of(k, LT - 1, LT))).astype(BF16)
+            send(md.at[k], mp.at[k], mds.at[k], mdr.at[k], (other, row, col))
+            return 0
+
+        lax.fori_loop(0, KB, to_modes, 0)
+
+        def mix_own(k, _):
+            acc[k] = dot(md[k], mw[pl.ds(pl.multiple_of(me * C, C), C), :])
+            return 0
+
+        lax.fori_loop(0, KB, mix_own, 0)
+
+        def mix(k, _):
+            drain(mp.at[k], mdr.at[k])
+            mixed = acc[k] + dot(mp[k], mw[pl.ds(pl.multiple_of(other * C, C), C), :])
+            ms[k] = (mixed * filt[...]).astype(BF16)
+            return 0
+
+        lax.fori_loop(0, KB, mix, 0)
+
+        for t in range(LT):
+            def to_synth(k, _, t=t):
+                basis = ib[k].reshape(NR, LT, NC, DEG)[:, t].reshape(ND, DEG)
+                got = dot(basis, ms[k])
+                for h in range(2):
+                    qf[pl.ds(k + 8 * h, ND, stride=16), :] = got[:, h * 128 : (h + 1) * 128]
+                return 0
+
+            lax.fori_loop(0, KB, to_synth, 0)
+
+            def narrow(i, _, t=t):
+                rows = pl.ds(pl.multiple_of(i * TB, TB), TB)
+                in_rows = pl.ds(pl.multiple_of(i * TB * 16, TB * 16), TB * 16)
+                qb[t, rows] = qf[in_rows, :].reshape(TB, 16, 128).astype(BF16)
+                return 0
+
+            lax.fori_loop(0, ND // TB, narrow, 0)
+            pltpu.make_async_copy(qb.at[t, flat], vx.at[t, flat], q_r.at[t]).start()
+
+            def gather_back(p, _, t=t):
+                r_to, c_to = partner(p)
+                send(qb.at[t, r_to * NC + c_to], vx.at[t, flat], q_s.at[t], q_r.at[t], (me, r_to, c_to))
+                return 0
+
+            lax.fori_loop(1, ND, gather_back, 0)
 
         drain(hd.at[0], hdr)
+        drain(fx.at[0:HO], fxr)
         drain(w2, ld.at[9])
 
         def conv_second(i, _):
@@ -480,65 +613,6 @@
         lax.fori_loop(0, WY // 2, conv_second, 0)
         pltpu.make_async_copy(oo, ocean_out, outs.at[0]).start()
 
-        drain(fb, ld.at[3])
-        for t in range(LT):
-            drain(rx.at[0:ND], r2.at[t])
-        TB = 32 if NLAT % 32 == 0 else 8
-
-        def widen(i, _):
-            rows = pl.ds(pl.multiple_of(i * TB, TB), TB)
-            out_rows = pl.ds(pl.multiple_of(i * TB * 16, TB * 16), TB * 16)
-            rxf[out_rows, :] = rx[rows].astype(F32).reshape(TB * 16, 128)
-            return 0
-
-        lax.fori_loop(0, NLAT // TB, widen, 0)
-
-        def to_modes(k, _):
-            col_k = jnp.concatenate(
-                [rxf[pl.ds(k + 8 * h, NLAT, stride=16), :] for h in range(2)], axis=1
-            ).astype(BF16)
-            md[k] = dot(fb[k], col_k).astype(BF16)
-            send(md.at[k], mp.at[k], mds.at[k], mdr.at[k], (other, row, col))
-            return 0
-
-        lax.fori_loop(0, KB, to_modes, 0)
-        drain(ib, ld.at[4])
-        drain(mw, ld.at[5])
-        drain(filt, ld.at[6])
-
-        def to_synth(k, _):
-            drain(mp.at[k], mdr.at[k])
-            mixed = dot(md[k], mw[pl.ds(pl.multiple_of(me * C, C), C), :])
-            mixed = mixed + dot(mp[k], mw[pl.ds(pl.multiple_of(other * C, C), C), :])
-            mixed = (mixed * filt[...]).astype(BF16)
-            got = dot(ib[k], mixed)
-            for h in range(2):
-                qf[pl.ds(k + 8 * h, NLAT, stride=16), :] = got[:, h * 128 : (h + 1) * 128]
-            return 0
-
-        lax.fori_loop(0, KB, to_synth, 0)
-
-        def narrow(i, _):
-            rows = pl.ds(pl.multiple_of(i * TB, TB), TB)
-            in_rows = pl.ds(pl.multiple_of(i * TB * 16, TB * 16), TB * 16)
-            qb[rows] = qf[in_rows, :].reshape(TB, 16, 128).astype(BF16)
-            return 0
-
-        lax.fori_loop(0, NLAT // TB, narrow, 0)
-
-        for t in range(LT):
-            pltpu.make_async_copy(qb.at[flat * LT + t], vx.at[t, flat], q_r.at[t]).start()
-
-            def gather_back(p, _, t=t):
-                r_to = rmod(row + p // NC)
-                c_to = shifted(lax.rem(p, NC) // NX, lax.rem(p, NX))
-                send(
-                    qb.at[(r_to * NC + c_to) * LT + t], vx.at[t, flat], q_s.at[t], q_r.at[t], (me, r_to, c_to)
-                )
-                return 0
-
-            lax.fori_loop(1, ND, gather_back, 0)
-
         drain(tab, ld.at[7])
         for t in range(LT):
             drain(vx.at[t], q_r.at[t])
@@ -547,34 +621,33 @@
                 bx[:, h * 128 : (h + 1) * 128] = part.astype(BF16)
 
             def synthesise(b, _, t=t):
-                rows = pl.ds(pl.multiple_of(b * FB, FB), FB)
+                y = lax.rem(col // NX + b, NY)
+                rows = pl.ds(pl.multiple_of(y * NX * PM, NX * PM), NX * PM)
                 gs[t, rows, :] = dot(tab[rows, :], bx[...]).astype(BF16)
-                return 0
-
-            lax.fori_loop(0, 4, synthesise, 0)
-            pltpu.make_async_copy(
-                gs.at[t, pl.ds(col * PM, PM)], hh.at[col * LT + t], gsr.at[t]
-            ).start()
-
-            def home(p, _, t=t):
-                there = shifted(p // NX, lax.rem(p, NX))
-                send(
-                    gs.at[t, pl.ds(there * PM, PM)], hh.at[col * LT + t], gss.at[t], gsr.at[t], (me, row, there)
-                )
-                return 0
-
-            lax.fori_loop(1, NC, home, 0)
+
+                def home(p, _):
+                    there = y * NX + lax.rem(lax.rem(col, NX) + p, NX)
+
+                    @pl.when(there != col)
+                    def _():
+                        send(gs.at[t, pl.ds(there * PM, PM)], grid_out.at[t * NC + col], gss.at[t], gsr.at[t],
+                             (me, row, there))
+
+                    @pl.when(there == col)
+                    def _():
+                        pltpu.make_async_copy(
+                            gs.at[t, pl.ds(col * PM, PM)], grid_out.at[t * NC + col], gsr.at[t]
+                        ).start()
+
+                    return 0
+
+                lax.fori_loop(0, NX, home, 0)
+                return 0
+
+            lax.fori_loop(0, NY, synthesise, 0)
 
         for t in range(LT):
-            drain(hh.at[0:NC], gsr.at[t])
-
-            def finish(c, _, t=t):
-                i = c * LT + t
-                lf[i] = (lf[i].astype(F32) + gelu(hh[i].astype(F32))).astype(BF16)
-                return 0
-
-            lax.fori_loop(0, NC, finish, 0)
-        pltpu.make_async_copy(lf, atm_out, outs.at[1]).start()
+            drain(grid_out.at[0:NC], gsr.at[t])
 
         for t in range(LT):
             drain(g1.at[t, 0 : (NC - 1) * PM], g1s.at[t])
@@ -582,6 +655,13 @@
             drain(vx.at[t, 0 : ND - 1], q_s.at[t])
             drain(gs.at[t, 0 : (NC - 1) * PM], gss.at[t])
         drain(sr.at[0 : NC - 1], sss)
+
+        @pl.when((col < me * HC) | (col >= me * HC + HC))
+        def _():
+            drain(sr.at[0], sss)
+
+        drain(ss.at[0:HC], shs)
+        drain(fx.at[0:HO], fxs)
         for q in range(2):
             for n, (there, src, dst, dev) in enumerate(water_sends(q)):
                 @pl.when(there)
@@ -602,12 +682,14 @@
     v = pltpu.VMEM
     dma = pltpu.SemaphoreType.DMA
     scratch = [
+        v((WY, WX), jnp.int32), v((WY, 4, WX), jnp.int32), v((WY, 4, WX), F32), v((PT, 4, PM), jnp.int32),
+        v((PT, 4, PM), F32), v((NF, C), BF16), v((NF, CO), BF16), v((NF, CO), BF16), v((NF, C), BF16),
         v((PT, PM, C), BF16), v((LT, NLON, C), BF16), v((NLON, NLON), BF16), v((NLON, NLON), BF16),
-        v((LT, ND, 16, 128), BF16), v((NLAT, 16, 128), BF16), v((NLAT * 16, 128), F32),
+        v((LT, ND, 16, 128), BF16), v((LT, ND, 16, 128), BF16), v((NLAT * 16, 128), F32),
         v((KB, DEG, NLAT), BF16), v((KB, NLAT, DEG), BF16), v((KB, DEG, C), BF16), v((KB, DEG, C), BF16),
-        v((2 * C, C), BF16), v((DEG, C), F32), v((NLAT * 16, 128), F32), v((NLAT, 16, 128), BF16),
+        v((2 * C, C), BF16), v((DEG, C), F32), v((ND * 16, 128), F32), v((LT, ND, 16, 128), BF16),
         v((LT, ND, 16, 128), BF16), v((NLON, C), BF16), v((LT, NLON, C), BF16), v((PT, PM, C), BF16),
-        v((PT, PM, C), BF16),
+        v((KB, DEG, NLAT), BF16), v((KB, DEG, C), F32), v((KB, DEG, C), BF16),
         v((2, XR, WP, CO), BF16), v((2, XR, 16, CO), BF16), v((2, XR, 16, CO), BF16), v((2, HR_, WP, CO), BF16),
         v((6 * CO, 3 * CO), BF16), v((6 * CO, 3 * CO), BF16), v((WY, WX, CO), BF16),
         v((NC, LANES, C), F32),
@@ -616,20 +698,20 @@
         v((16, AR * NF), BF16), v((16, AR * NF), BF16), v((16, OR * NF), BF16), v((16, OR * NF), BF16),
         v((4, LANES), F32), v((4, LANES), F32), v((4, LANES), F32),
         v((NC, NF, LANES), BF16), v((NC, NF, LANES), BF16), v((WY // 2, NF, LANES), BF16),
-        dma((10,)), dma((9, 2)), dma((9, 2)), dma((2,)), dma((2,)), dma((8,)), dma((8,)),
+        dma((19,)), dma((9, 2)), dma((9, 2)), dma((2,)), dma((2,)), dma((8,)), dma((8,)),
         dma((LT,)), dma((LT,)), dma, dma, dma((LT,)), dma((LT,)), dma((KB,)), dma((KB,)),
-        dma((LT,)), dma((LT,)), dma((LT,)), dma((LT,)), dma, dma, dma((2,)), pltpu.SemaphoreType.REGULAR,
+        dma((LT,)), dma((LT,)), dma((LT,)), dma((LT,)), dma, dma, dma((2,)), dma, dma, dma, dma, pltpu.SemaphoreType.REGULAR,
     ]
     any_ = pl.BlockSpec(memory_space=pl.ANY)
-    vm = pl.BlockSpec(memory_space=pltpu.VMEM)
     return pl.pallas_call(
         kernel,
         out_shape=(
             jax.ShapeDtypeStruct((PT, PM, C), BF16),
+            jax.ShapeDtypeStruct((PT, PM, C), BF16),
             jax.ShapeDtypeStruct((WY, WX, CO), BF16),
         ),
-        in_specs=[any_, any_] + [vm] * 9 + [any_] * 8,
-        out_specs=(any_, any_),
+        in_specs=[any_] * 19,
+        out_specs=(any_, any_, any_),
         scratch_shapes=scratch,
         compiler_params=pltpu.CompilerParams(
             collective_id=0, has_side_effects=True, vmem_limit_bytes=60 * 1024 * 1024
@@ -655,7 +737,7 @@
         step = make_kernel(
             NR, NC, NX, PT, PM, C, WY, WX, CO, flux_weight.shape[1], forward_basis.shape[1]
         )
-        return step(
+        lifted, grid, ocean_out = step(
             atmosphere_state,
             water_condition,
             ocean_cell_mask,
@@ -676,6 +758,8 @@
             jnp.asarray(table),
             jnp.asarray(np.ascontiguousarray(table.T)),
         )
+        atm_out = (lifted.astype(F32) + gelu(grid.astype(F32))).astype(BF16)
+        return atm_out, ocean_out
 
     placed = (
         P("row", "col", "comp"),

time: 153 us -> 139 us (0.908)
  Pallas kernels: 147 us -> 133 us
  other arithmetic: 0 us -> 4.37 us
  local copies, waits for them, and re-layouts: 3.68 us -> 0.88 us
    pallas_call x1, Pallas kernels: 147 us -> 133 us  [local(): step(atmosphere_state, water_condition, ocean_cell_mask, jnp.swapaxes(atm...]
    convert_element_type x0 -> x1, other arithmetic: none -> 4.37 us  [local(): atm_out = (lifted.astype(F32) + gelu(grid.astype(F32))).astype(BF16)]
    unnamed x4 -> x3, local copies, waits for them, and re-layouts: 3.68 us -> 0.88 us
where the time goes in v1:
time: 139 us
  Pallas kernels  133 us (96%)
  other arithmetic  4.37 us (3%)
    pallas_call x1, Pallas kernels, local(): step(atmosphere_state, water_condition, ocean_cell_mask, jnp.swapaxes(atm...  133 us
    convert_element_type x1, other arithmetic, local(): atm_out = (lifted.astype(F32) + gelu(grid.astype(F32))).astype(BF16)  4.37 us

profile of v1, /device:TPU:8, one launch (start us, length us, event | category | flops | bytes accessed | tf_op | source)
XLA Modules:
  0.0 138.7 jit_solution(13825562985318444640)
XLA Ops:
  0.6 132.8 %coupled_step.1 = (bf16[48,64,256]{2,1,0:T(8,128)(2,1)}, bf16[48,64,256]{2,1,0:T(8,128)(2,1)}, bf16[24,128,128]{2,1,0:T(8,128)(2,1)}) custom-call(bf16[48,64,256]{2,1,0:T(8,128)(2,1)} %atm.1, bf16[24,128,128]{2,1,0:T(8,128)(2,1)} %water.1, s32[24,128]{1,0:T(8,128)} %mask_h.1, s32[24,4,128]{2,1,0:T(4,128)} %bitcast.8, f32[24,4,128]{2,1,0:T(4,128)} %bitcast.9, ...), custom_call_target="tpu_custom_call" | custom-call | flops 8999999488 | bytes 20000000 | tf_op jit(solution)/shard_map/coupled_step/pallas_call | solution.py:740
  133.5 0.0 copy-start
  133.5 4.4 %fusion.6 = bf16[48,64,256]{2,1,0:T(8,128)(2,1)} fusion(bf16[48,64,256]{2,1,0:T(8,128)(2,1)} %get-tuple-element.6, bf16[48,64,256]{2,1,0:T(8,128)(2,1)} %get-tuple-element.5), kind=kLoop, calls=%fused_computation.10 | loop fusion | flops 9437184 | bytes 4718592 | tf_op jit(solution)/shard_map/convert_element_type | solution.py:761
  137.9 0.0 copy-done
  137.9 0.9 copy.22
Async XLA Ops:
  133.5 4.4 %copy-start = (bf16[24,128,128]{2,1,0:T(8,128)(2,1)S(1)}, bf16[24,128,128]{2,1,0:T(8,128)(2,1)}, u32[]{:S(2)}) copy-start(bf16[24,128,128]{2,1,0:T(8,128)(2,1)} %get-tuple-element.11) | copy-start | bytes 2359300

commit v2 on v1

--- a/solution.py
+++ b/solution.py
@@ -52,7 +52,7 @@
     KB = NLON // ND
     NLAT = NR * PT
     NY = NC // NX
-    HC, HO = NC // 2, WY // 4
+    HC, HO, W8 = NC // 2, WY // 4, WY // 8
     AR, AC = PT + 2, PM + 2
     OR, OC = WY + 2, WX + 2
     WP = WX + 16
@@ -62,10 +62,10 @@
 
     def kernel(
         atm, water, mask_h, oidx_h, ow_h, aidx_h, aw_h, fwt_h, flw_h, ipmt_h, drv_h, fb_h, ib_h, mw_h, filt_h,
-        k1_h, k2_h, tab_h, tabt_h, lifted_out, grid_out, ocean_out,
-        mask, oidx, ow, aidx, aw, fwt, flw, ipmt, drv,
-        atm_v, g1, tabt, tab, sp, rx, rxf, fb, ib, md, mp, mw, filt, qf, qb, vx, bx, gs, lf, fbp, acc, ms,
-        x, hl, hr, hd, w1, w2, oo, dsc,
+        k1_h, k2_h, tab_h, tabt_h, atm_out, ocean_out,
+        mask, oidx, ow, aidx, aw, fwt, flw, ipmt, drv, ya, us, st, drv3, wl, wr,
+        atm_v, g1, tabt, tab, sp, rx, rxf, fb, ib, md, mp, mw, filt, qf, qb, vx, bx, gs, hh, lf, fbp, acc, ms,
+        x, hl, hr, hd, w1, w2, oo,
         tf, ts, pf, ps, ef, es, efl, efr, esl, esr, rsc, csc, wsc, ss, sr, fx,
         ld, wsend, wrecv, csend, crecv, hsend, hrecv, g1s, g1r, sss, ssr, s2s, r2, mds, mdr,
         q_s, q_r, gss, gsr, hds, hdr, outs, shs, shr, fxs, fxr, ready,
@@ -146,6 +146,21 @@
             return 0
 
         lax.fori_loop(0, WY // 4, project_water, 0)
+        sub = lax.broadcasted_iota(jnp.int32, (16, CO), 0)
+
+        def pack_edges(j, _):
+            left = jnp.zeros((16, CO), F32)
+            right = jnp.zeros((16, CO), F32)
+            for m in range(8):
+                mine = (sub >= 2 * m) & (sub < 2 * m + 2)
+                head = x[me, 2 + 8 * j + m, 0:16, :].astype(F32)
+                tail = x[me, 2 + 8 * j + m, WX - 16 : WX, :].astype(F32)
+                left = jnp.where(mine, pltpu.roll(head, 2 * m, 0), left)
+                right = jnp.where(mine, pltpu.roll(tail, (2 * m + 2) % 16, 0), right)
+            wl[j] = left.astype(BF16)
+            wr[j] = right.astype(BF16)
+            return 0
+
         pl.semaphore_wait(barrier, NC - 1 + NR - 1 + 9 + 4)
         for d in range(1, NR):
             pl.semaphore_signal(ready, inc=1, device_id=(me, rmod(row + d), col), device_id_type=MESH)
@@ -168,15 +183,12 @@
             return [
                 (row > 0, water.at[0:2], x.at[me, XR - 2 : XR, 0:WX], (q, rmod(row - 1), col)),
                 (row < NR - 1, water.at[WY - 2 : WY], x.at[me, 0:2, 0:WX], (q, rmod(row + 1), col)),
-                (col > 0, water.at[:, 0:16], hr.at[me, 2 : 2 + WY], (q, row, cmod(col - 1))),
-                (col < NC - 1, water.at[:, WX - 16 : WX], hl.at[me, 2 : 2 + WY], (q, row, cmod(col + 1))),
-                ((row > 0) & (col > 0), water.at[0:2, 0:16], hr.at[me, XR - 2 : XR],
-                 (q, rmod(row - 1), cmod(col - 1))),
-                ((row > 0) & (col < NC - 1), water.at[0:2, WX - 16 : WX], hl.at[me, XR - 2 : XR],
-                 (q, rmod(row - 1), cmod(col + 1))),
-                ((row < NR - 1) & (col > 0), water.at[WY - 2 : WY, 0:16], hr.at[me, 0:2],
-                 (q, rmod(row + 1), cmod(col - 1))),
-                ((row < NR - 1) & (col < NC - 1), water.at[WY - 2 : WY, WX - 16 : WX], hl.at[me, 0:2],
+                (col > 0, wl, hr.at[me, 0:W8], (q, row, cmod(col - 1))),
+                (col < NC - 1, wr, hl.at[me, 0:W8], (q, row, cmod(col + 1))),
+                ((row > 0) & (col > 0), wl.at[0], hr.at[me, W8 + 1], (q, rmod(row - 1), cmod(col - 1))),
+                ((row > 0) & (col < NC - 1), wr.at[0], hl.at[me, W8 + 1], (q, rmod(row - 1), cmod(col + 1))),
+                ((row < NR - 1) & (col > 0), wl.at[W8 - 1], hr.at[me, W8], (q, rmod(row + 1), cmod(col - 1))),
+                ((row < NR - 1) & (col < NC - 1), wr.at[W8 - 1], hl.at[me, W8],
                  (q, rmod(row + 1), cmod(col + 1))),
             ]
 
@@ -184,12 +196,12 @@
             return [
                 (row < NR - 1, x.at[q, XR - 2 : XR, 0:WX]),
                 (row > 0, x.at[q, 0:2, 0:WX]),
-                (col < NC - 1, hr.at[q, 2 : 2 + WY]),
-                (col > 0, hl.at[q, 2 : 2 + WY]),
-                ((row < NR - 1) & (col < NC - 1), hr.at[q, XR - 2 : XR]),
-                ((row < NR - 1) & (col > 0), hl.at[q, XR - 2 : XR]),
-                ((row > 0) & (col < NC - 1), hr.at[q, 0:2]),
-                ((row > 0) & (col > 0), hl.at[q, 0:2]),
+                (col < NC - 1, hr.at[q, 0:W8]),
+                (col > 0, hl.at[q, 0:W8]),
+                ((row < NR - 1) & (col < NC - 1), hr.at[q, W8 + 1]),
+                ((row < NR - 1) & (col > 0), hl.at[q, W8 + 1]),
+                ((row > 0) & (col < NC - 1), hr.at[q, W8]),
+                ((row > 0) & (col > 0), hl.at[q, W8]),
             ]
 
         send_lat(0)
@@ -202,20 +214,6 @@
                         send(src, dst, wsend.at[first + n, q], wrecv.at[first + n, me], dev)
 
         water_send(0, 2)
-        drain(atm_v, ld.at[0])
-        drain(fwt, ld.at[11])
-
-        def project_air(t, _):
-            cells = atm_v[pl.ds(t * 4, 4)].reshape(4 * PM, C)
-            got = dot_nt(fwt[...], cells)
-            zeros = jnp.zeros((NF, 128 - PM), F32)
-            for j in range(4):
-                part = jnp.concatenate([got[:, j * PM : (j + 1) * PM], zeros], axis=1)
-                pf[me, pl.ds((t * 4 + j) * NF, NF), :] = part.astype(BF16)
-            return 0
-
-        lax.fori_loop(0, PT // 4, project_air, 0)
-        send(pf.at[me], pf.at[me], csend.at[1], crecv.at[1], (other, row, col))
 
         def both(part):
             return (part[0].astype(F32) + part[1].astype(F32)).astype(BF16)
@@ -226,82 +224,60 @@
         def pick(cond):
             return jnp.where(cond, 1.0, 0.0).astype(BF16)
 
-        def row_halo_send(tab_ref, rows, at):
+        def halo_parts(tab_ref, edge, left, right, rows):
             above = pl.ds((rows + 1) * NF, NF)
             below = pl.ds(rows * NF, NF)
-
-            @pl.when(row > 0)
-            def _():
-                send(tab_ref.at[0:NF, 0:128], tab_ref.at[below, 0:128], hsend.at[at], hrecv.at[at],
-                     (me, rmod(row - 1), col))
-
-            @pl.when(row < NR - 1)
-            def _():
-                send(tab_ref.at[(rows - 1) * NF : rows * NF, 0:128], tab_ref.at[above, 0:128],
-                     hsend.at[at + 1], hrecv.at[at + 1], (me, rmod(row + 1), col))
-
-        def row_halo_recv(tab_ref, rows, at):
-            above = pl.ds((rows + 1) * NF, NF)
-            below = pl.ds(rows * NF, NF)
-
-            @pl.when(row < NR - 1)
-            def _():
-                drain(tab_ref.at[below, 0:128], hrecv.at[at])
+            parts = [
+                (row > 0, row < NR - 1, tab_ref.at[0:NF, 0:128], tab_ref.at[below, 0:128], (-1, 0)),
+                (row < NR - 1, row > 0, tab_ref.at[(rows - 1) * NF : rows * NF, 0:128], tab_ref.at[above, 0:128],
+                 (1, 0)),
+            ]
+            for dr in (-1, 0, 1):
+                to = (row > 0) if dr < 0 else (row < NR - 1) if dr > 0 else (row >= 0)
+                fro = (row < NR - 1) if dr < 0 else (row > 0) if dr > 0 else (row >= 0)
+                parts.append((to & (col > 0), fro & (col < NC - 1), edge, right.at[1 - dr], (dr, -1)))
+                parts.append((to & (col < NC - 1), fro & (col > 0), edge, left.at[1 - dr], (dr, 1)))
+            return parts
+
+        def halo_send(tab_ref, edge, left, right, rows, width, at):
+            ends = pick(((line == 0) & (lane == 0)) | ((line == 1) & (lane == width - 1)))
+            edge[...] = dot_nt(ends, tab_ref[0 : rows * NF, 0:128]).astype(BF16)
+            for n, (to, _, src, dst, (dr, dc)) in enumerate(halo_parts(tab_ref, edge, left, right, rows)):
+                @pl.when(to)
+                def _(src=src, dst=dst, n=n, dr=dr, dc=dc):
+                    send(src, dst, hsend.at[at + n], hrecv.at[at + n], (me, rmod(row + dr), cmod(col + dc)))
+
+        def halo_recv(tab_ref, edge, left, right, rows, at):
+            for n, (_, fro, src, dst, _) in enumerate(halo_parts(tab_ref, edge, left, right, rows)):
+                @pl.when(fro)
+                def _(dst=dst, n=n):
+                    drain(dst, hrecv.at[at + n])
 
             @pl.when(row == NR - 1)
             def _():
-                tab_ref[below, 0:128] = jnp.zeros((NF, 128), BF16)
-
-            @pl.when(row > 0)
-            def _():
-                drain(tab_ref.at[above, 0:128], hrecv.at[at + 1])
+                tab_ref[rows * NF : (rows + 1) * NF, 0:128] = jnp.zeros((NF, 128), BF16)
 
             @pl.when(row == 0)
             def _():
-                tab_ref[above, 0:128] = jnp.zeros((NF, 128), BF16)
-
-        def sent(cond, ref, at):
-            @pl.when(cond)
-            def _():
-                drain(ref, hsend.at[at])
-
-        def row_halo_sent(tab_ref, at):
-            sent(row > 0, tab_ref.at[0:NF, 0:128], at)
-            sent(row < NR - 1, tab_ref.at[0:NF, 0:128], at + 1)
-
-        def col_halo_send(tab_ref, edge, left, right, width, at):
-            ends = pick(((line == 0) & (lane == 0)) | ((line == 1) & (lane == width - 1)))
-            edge[...] = dot_nt(ends, tab_ref[:, 0:128]).astype(BF16)
-
-            @pl.when(col > 0)
-            def _():
-                send(edge, right, hsend.at[at], hrecv.at[at], (me, row, cmod(col - 1)))
-
-            @pl.when(col < NC - 1)
-            def _():
-                send(edge, left, hsend.at[at + 1], hrecv.at[at + 1], (me, row, cmod(col + 1)))
-
-        def col_halo_recv(left, right, at):
-            @pl.when(col < NC - 1)
-            def _():
-                drain(right, hrecv.at[at])
-
-            @pl.when(col == NC - 1)
-            def _():
-                right[...] = jnp.zeros(right.shape, BF16)
-
-            @pl.when(col > 0)
-            def _():
-                drain(left, hrecv.at[at + 1])
-
-            @pl.when(col == 0)
-            def _():
-                left[...] = jnp.zeros(left.shape, BF16)
-
-        def halo_columns(left, right, place):
+                tab_ref[(rows + 1) * NF : (rows + 2) * NF, 0:128] = jnp.zeros((NF, 128), BF16)
+
+        def halo_sent(tab_ref, edge, left, right, rows, at, first, last):
+            for n, (to, _, src, _, _) in enumerate(halo_parts(tab_ref, edge, left, right, rows)):
+                if first <= n < last:
+                    @pl.when(to)
+                    def _(src=src, n=n):
+                        drain(src, hsend.at[at + n])
+
+        def halo_columns(left, right, rows, place):
+            def column(got, inside):
+                mid = jnp.where(inside, got[1].astype(F32), 0.0)
+                below = jnp.where(inside & (row < NR - 1), got[2].astype(F32)[:, 0:NF], 0.0)
+                above = jnp.where(inside & (row > 0), got[0].astype(F32)[:, (rows - 1) * NF : rows * NF], 0.0)
+                return jnp.concatenate([mid, below, above], axis=1).astype(BF16)
+
             from_right = pick((line == 0) & (lane == place))
             from_left = pick((line == 1) & (lane == place + 1))
-            return dot_tn(right[...], from_right) + dot_tn(left[...], from_left)
+            return dot_tn(column(right, col < NC - 1), from_right) + dot_tn(column(left, col > 0), from_left)
 
         def regrid(tab_ref, index, weight, rows, cols, block):
             cells = index.astype(F32)
@@ -329,19 +305,27 @@
 
         drain(ps.at[0], crecv.at[0])
         ts[0 : WY * NF, 0:128] = both(ps)
-        row_halo_send(ts, WY, 0)
-        row_halo_recv(ts, WY, 0)
-        col_halo_send(ts, es, esl, esr, WX, 4)
+        halo_send(ts, es, esl, esr, WY, WX, 0)
+
+        drain(atm_v, ld.at[0])
+        drain(fwt, ld.at[11])
+
+        def project_air(t, _):
+            cells = atm_v[pl.ds(t * 4, 4)].reshape(4 * PM, C)
+            got = dot_nt(fwt[...], cells)
+            zeros = jnp.zeros((NF, 128 - PM), F32)
+            for j in range(4):
+                part = jnp.concatenate([got[:, j * PM : (j + 1) * PM], zeros], axis=1)
+                pf[me, pl.ds((t * 4 + j) * NF, NF), :] = part.astype(BF16)
+            return 0
+
+        lax.fori_loop(0, PT // 4, project_air, 0)
+        send(pf.at[me], pf.at[me], csend.at[1], crecv.at[1], (other, row, col))
+
         send_lat(1)
-        send(water, x.at[me, 2 : 2 + WY, 0:WX], wsend.at[8, 0], wrecv.at[8, 0], (other, row, col))
-
-        drain(pf.at[0], crecv.at[1])
-        tf[0 : PT * NF, :] = both(pf)
-        row_halo_send(tf, PT, 2)
-
-        col_halo_recv(esl, esr, 4)
-        row_halo_sent(ts, 0)
-        ts[:, 128:256] = halo_columns(esl, esr, 0).astype(BF16)
+        halo_recv(ts, es, esl, esr, WY, 0)
+        halo_sent(ts, es, esl, esr, WY, 0, 0, 2)
+        ts[:, 128:256] = halo_columns(esl, esr, WY, 0).astype(BF16)
 
         for n, ref in ((12, aidx), (13, aw), (14, drv)):
             drain(ref, ld.at[n])
@@ -370,39 +354,51 @@
 
         lax.fori_loop(0, HC, to_air, 0)
         send_lat(2)
+        lax.fori_loop(0, W8, pack_edges, 0)
         water_send(2, 8)
+        send(water, x.at[me, 2 : 2 + WY, 0:WX], wsend.at[8, 0], wrecv.at[8, 0], (other, row, col))
+        drain(pf.at[0], crecv.at[1])
+        tf[0 : PT * NF, :] = both(pf)
+        halo_send(tf, ef, efl, efr, PT, PM, 8)
 
         drain(tabt, ld.at[2])
-        drain(sr, ssr)
-
-        def lift_terms(c, _):
-            dsc[c] = dot_tn(sr[c], drv[...])
-            return 0
-
-        lax.fori_loop(0, NC, lift_terms, 0)
-
-        pl.semaphore_wait(ready, NR - 1)
 
         for t in range(LT):
             drain(g1.at[t], g1r.at[t])
 
-            def lift_lat(c, _, t=t):
-                rows = pl.ds(pl.multiple_of(c * PM, PM), PM)
-                g1[t, rows, :] = (
-                    g1[t, rows, :].astype(F32) + dsc[c, t * PM : (t + 1) * PM, :]
-                ).astype(BF16)
-                return 0
-
-            lax.fori_loop(0, NC, lift_lat, 0)
-
             def analyse(b, _, t=t):
                 rows = pl.ds(pl.multiple_of(b * FB, FB), FB)
-                got = dot(tabt[rows, :], g1[t])
+                ya[t, rows, :] = dot(tabt[rows, :], g1[t])
+                return 0
+
+            lax.fori_loop(0, 4, analyse, 0)
+
+        drv3[...] = jnp.zeros(drv3.shape, BF16)
+        for t in range(LT):
+            drv3[t, t * NF : (t + 1) * NF, :] = drv[...]
+        drain(sr, ssr)
+        for t in range(LT):
+            st[t * NF : (t + 1) * NF, :] = jnp.concatenate(
+                [sr[c].astype(F32)[:, t * PM : (t + 1) * PM] for c in range(NC)], axis=1
+            ).astype(BF16)
+
+        def analyse_fields(b, _):
+            rows = pl.ds(pl.multiple_of(b * FB, FB), FB)
+            us[rows, :] = dot_nt(tabt[rows, :], st[...]).astype(BF16)
+            return 0
+
+        lax.fori_loop(0, 4, analyse_fields, 0)
+        pl.semaphore_wait(ready, NR - 1)
+
+        for t in range(LT):
+            def force(b, _, t=t):
+                rows = pl.ds(pl.multiple_of(b * FB, FB), FB)
+                got = ya[t, rows, :] + dot(us[rows, :], drv3[t])
                 halves = [got[:, h * 128 : (h + 1) * 128].reshape(FB // 8, 8, 128) for h in range(2)]
                 sp[t, pl.ds(b * (FB // 8), FB // 8)] = jnp.concatenate(halves, axis=1).astype(BF16)
                 return 0
 
-            lax.fori_loop(0, 4, analyse, 0)
+            lax.fori_loop(0, 4, force, 0)
             pltpu.make_async_copy(sp.at[t, flat], rx.at[t, flat], r2.at[t]).start()
 
             def scatter(p, _, t=t):
@@ -422,7 +418,6 @@
             return 0
 
         lax.fori_loop(0, NC, lift_here, 0)
-        pltpu.make_async_copy(lf, lifted_out, outs.at[1]).start()
 
         drain(fb, ld.at[3])
         lat_in = lax.broadcasted_iota(jnp.int32, (NLAT, NLAT), 0)
@@ -435,9 +430,6 @@
             return 0
 
         lax.fori_loop(0, KB, reorder, 0)
-
-        row_halo_recv(tf, PT, 2)
-        col_halo_send(tf, ef, efl, efr, PM, 6)
 
         for q in range(2):
             for n, (there, dst) in enumerate(water_recvs(q)):
@@ -454,16 +446,26 @@
         def _():
             x[:, XR - 2 : XR, 0:WX, :] = jnp.zeros((2, 2, WX, CO), BF16)
 
-        def side(i, _):
-            inside = ((i >= 2) | (row > 0)) & ((i < XR - 2) | (row < NR - 1))
-            sub = lax.broadcasted_iota(jnp.int32, (16, CO), 0)
+        def side(i, tile, m, inside):
             for q in range(2):
-                from_right = jnp.where((sub < 2) & inside & (col < NC - 1), hr[q, i].astype(F32), 0.0)
-                from_left = jnp.where((sub >= 14) & inside & (col > 0), hl[q, i].astype(F32), 0.0)
-                x[q, i, WX:WP, :] = (from_right + from_left).astype(BF16)
-            return 0
-
-        lax.fori_loop(0, XR, side, 0)
+                from_right = pltpu.roll(hr[q, tile].astype(F32), (16 - 2 * m) % 16, 0)
+                from_left = pltpu.roll(hl[q, tile].astype(F32), (30 - 2 * m) % 16, 0)
+                cells = jnp.where(
+                    (sub < 2) & inside & (col < NC - 1),
+                    from_right,
+                    jnp.where((sub >= 14) & inside & (col > 0), from_left, 0.0),
+                )
+                x[q, i, WX:WP, :] = cells.astype(BF16)
+
+        def sides(j, _):
+            for m in range(8):
+                side(2 + 8 * j + m, j, m, True)
+            return 0
+
+        lax.fori_loop(0, W8, sides, 0)
+        for m in range(2):
+            side(m, W8, 6 + m, row > 0)
+            side(XR - 2 + m, W8 + 1, m, row < NR - 1)
         drain(w1, ld.at[8])
 
         def taps(src, weight, first, count):
@@ -497,9 +499,9 @@
         lax.fori_loop(0, HR_ // 2, conv_first, 0)
         send(hd.at[me], hd.at[me], hds, hdr, (other, row, col))
 
-        col_halo_recv(efl, efr, 6)
-        row_halo_sent(tf, 2)
-        tf[...] = (tf[...].astype(F32) + halo_columns(efl, efr, PM)).astype(BF16)
+        halo_recv(tf, ef, efl, efr, PT, 8)
+        halo_sent(tf, ef, efl, efr, PT, 8, 0, 2)
+        tf[...] = (tf[...].astype(F32) + halo_columns(efl, efr, PT, PM)).astype(BF16)
 
         for n, ref in ((15, mask), (16, oidx), (17, ow), (18, flw)):
             drain(ref, ld.at[n])
@@ -630,13 +632,13 @@
 
                     @pl.when(there != col)
                     def _():
-                        send(gs.at[t, pl.ds(there * PM, PM)], grid_out.at[t * NC + col], gss.at[t], gsr.at[t],
+                        send(gs.at[t, pl.ds(there * PM, PM)], hh.at[t * NC + col], gss.at[t], gsr.at[t],
                              (me, row, there))
 
                     @pl.when(there == col)
                     def _():
                         pltpu.make_async_copy(
-                            gs.at[t, pl.ds(col * PM, PM)], grid_out.at[t * NC + col], gsr.at[t]
+                            gs.at[t, pl.ds(col * PM, PM)], hh.at[t * NC + col], gsr.at[t]
                         ).start()
 
                     return 0
@@ -647,7 +649,16 @@
             lax.fori_loop(0, NY, synthesise, 0)
 
         for t in range(LT):
-            drain(grid_out.at[0:NC], gsr.at[t])
+            drain(hh.at[t * NC : (t + 1) * NC], gsr.at[t])
+
+            def finish(c, _, t=t):
+                n = t * NC + c
+                lf[n] = (lf[n].astype(F32) + gelu(hh[n].astype(F32))).astype(BF16)
+                return 0
+
+            lax.fori_loop(0, NC, finish, 0)
+            done = pl.ds(t * NC, NC)
+            pltpu.make_async_copy(lf.at[done], atm_out.at[done], outs.at[1]).start()
 
         for t in range(LT):
             drain(g1.at[t, 0 : (NC - 1) * PM], g1s.at[t])
@@ -673,9 +684,8 @@
         drain(hd.at[0], hds)
         for k in range(KB):
             drain(mp.at[k], mds.at[k])
-        for at, edge in ((4, es), (6, ef)):
-            sent(col > 0, edge, at)
-            sent(col < NC - 1, edge, at + 1)
+        halo_sent(ts, es, esl, esr, WY, 0, 2, 8)
+        halo_sent(tf, ef, efl, efr, PT, 8, 2, 8)
         drain(oo, outs.at[0])
         drain(lf, outs.at[1])
 
@@ -684,21 +694,22 @@
     scratch = [
         v((WY, WX), jnp.int32), v((WY, 4, WX), jnp.int32), v((WY, 4, WX), F32), v((PT, 4, PM), jnp.int32),
         v((PT, 4, PM), F32), v((NF, C), BF16), v((NF, CO), BF16), v((NF, CO), BF16), v((NF, C), BF16),
+        v((LT, NLON, C), F32), v((NLON, LT * NF), BF16), v((LT * NF, NLON), BF16), v((LT, LT * NF, C), BF16),
+        v((W8, 16, CO), BF16), v((W8, 16, CO), BF16),
         v((PT, PM, C), BF16), v((LT, NLON, C), BF16), v((NLON, NLON), BF16), v((NLON, NLON), BF16),
         v((LT, ND, 16, 128), BF16), v((LT, ND, 16, 128), BF16), v((NLAT * 16, 128), F32),
         v((KB, DEG, NLAT), BF16), v((KB, NLAT, DEG), BF16), v((KB, DEG, C), BF16), v((KB, DEG, C), BF16),
         v((2 * C, C), BF16), v((DEG, C), F32), v((ND * 16, 128), F32), v((LT, ND, 16, 128), BF16),
-        v((LT, ND, 16, 128), BF16), v((NLON, C), BF16), v((LT, NLON, C), BF16), v((PT, PM, C), BF16),
+        v((LT, ND, 16, 128), BF16), v((NLON, C), BF16), v((LT, NLON, C), BF16), v((PT, PM, C), BF16), v((PT, PM, C), BF16),
         v((KB, DEG, NLAT), BF16), v((KB, DEG, C), F32), v((KB, DEG, C), BF16),
-        v((2, XR, WP, CO), BF16), v((2, XR, 16, CO), BF16), v((2, XR, 16, CO), BF16), v((2, HR_, WP, CO), BF16),
+        v((2, XR, WP, CO), BF16), v((2, W8 + 2, 16, CO), BF16), v((2, W8 + 2, 16, CO), BF16), v((2, HR_, WP, CO), BF16),
         v((6 * CO, 3 * CO), BF16), v((6 * CO, 3 * CO), BF16), v((WY, WX, CO), BF16),
-        v((NC, LANES, C), F32),
         v((AR * NF, 128), BF16), v((OR * NF, 256), BF16), v((2, PT * NF, 128), BF16), v((2, WY * NF, 128), BF16),
-        v((16, AR * NF), BF16), v((16, OR * NF), BF16),
-        v((16, AR * NF), BF16), v((16, AR * NF), BF16), v((16, OR * NF), BF16), v((16, OR * NF), BF16),
+        v((16, PT * NF), BF16), v((16, WY * NF), BF16),
+        v((3, 16, PT * NF), BF16), v((3, 16, PT * NF), BF16), v((3, 16, WY * NF), BF16), v((3, 16, WY * NF), BF16),
         v((4, LANES), F32), v((4, LANES), F32), v((4, LANES), F32),
         v((NC, NF, LANES), BF16), v((NC, NF, LANES), BF16), v((WY // 2, NF, LANES), BF16),
-        dma((19,)), dma((9, 2)), dma((9, 2)), dma((2,)), dma((2,)), dma((8,)), dma((8,)),
+        dma((19,)), dma((9, 2)), dma((9, 2)), dma((2,)), dma((2,)), dma((16,)), dma((16,)),
         dma((LT,)), dma((LT,)), dma, dma, dma((LT,)), dma((LT,)), dma((KB,)), dma((KB,)),
         dma((LT,)), dma((LT,)), dma((LT,)), dma((LT,)), dma, dma, dma((2,)), dma, dma, dma, dma, pltpu.SemaphoreType.REGULAR,
     ]
@@ -707,11 +718,10 @@
         kernel,
         out_shape=(
             jax.ShapeDtypeStruct((PT, PM, C), BF16),
-            jax.ShapeDtypeStruct((PT, PM, C), BF16),
             jax.ShapeDtypeStruct((WY, WX, CO), BF16),
         ),
         in_specs=[any_] * 19,
-        out_specs=(any_, any_, any_),
+        out_specs=(any_, any_),
         scratch_shapes=scratch,
         compiler_params=pltpu.CompilerParams(
             collective_id=0, has_side_effects=True, vmem_limit_bytes=60 * 1024 * 1024
@@ -719,6 +729,36 @@
         cost_estimate=pl.CostEstimate(flops=9_000_000_000, bytes_accessed=20_000_000, transcendentals=2_000_000),
         name="coupled_step",
     )
+
+
+def settle(*arrays):
+    pieces = 8 if all(a.shape[0] % 8 == 0 for a in arrays) else 4
+
+    def kernel(*refs):
+        count = len(arrays)
+        sems = refs[-1]
+        copies = []
+        for n in range(count):
+            step = arrays[n].shape[0] // pieces
+            for p in range(pieces):
+                part = pl.ds(p * step, step)
+                copies.append(
+                    pltpu.make_async_copy(refs[n].at[part], refs[count + n].at[part], sems.at[n, p])
+                )
+        for copy in copies:
+            copy.start()
+        for copy in copies:
+            copy.wait()
+
+    any_ = pl.BlockSpec(memory_space=pl.ANY)
+    return pl.pallas_call(
+        kernel,
+        out_shape=tuple(jax.ShapeDtypeStruct(a.shape, a.dtype) for a in arrays),
+        in_specs=[any_] * len(arrays),
+        out_specs=tuple([any_] * len(arrays)),
+        scratch_shapes=[pltpu.SemaphoreType.DMA((len(arrays), pieces))],
+        name="settle",
+    )(*arrays)
 
 
 def solution(mesh):
@@ -737,7 +777,7 @@
         step = make_kernel(
             NR, NC, NX, PT, PM, C, WY, WX, CO, flux_weight.shape[1], forward_basis.shape[1]
         )
-        lifted, grid, ocean_out = step(
+        return settle(*step(
             atmosphere_state,
             water_condition,
             ocean_cell_mask,
@@ -757,9 +797,7 @@
             second_ocean_kernel,
             jnp.asarray(table),
             jnp.asarray(np.ascontiguousarray(table.T)),
-        )
-        atm_out = (lifted.astype(F32) + gelu(grid.astype(F32))).astype(BF16)
-        return atm_out, ocean_out
+        ))
 
     placed = (
         P("row", "col", "comp"),

time: 139 us -> 208 us (1.50)
  Pallas kernels: 133 us -> 207 us
  other arithmetic: 4.37 us -> 0 us
    pallas_call x0 -> x1, Pallas kernels: none -> 72.7 us  [settle(): pl.pallas_call(kernel, out_shape=tuple((jax.ShapeDtypeStruct(a.shape, a.d...]
    convert_element_type x1 -> x0, other arithmetic: 4.37 us -> none  [local(): atm_out = (lifted.astype(F32) + gelu(grid.astype(F32))).astype(BF16)]
where the time goes in v2:
time: 208 us
  Pallas kernels  207 us (100%)
    pallas_call x1, Pallas kernels, local(): step(atmosphere_state, water_condition, ocean_cell_mask, jnp.swapaxes(atm...  134 us
    pallas_call x1, Pallas kernels, settle(): pl.pallas_call(kernel, out_shape=tuple((jax.ShapeDtypeStruct(a.shape, a.d...  72.7 us

profile of v2, /device:TPU:8, one launch (start us, length us, event | category | flops | bytes accessed | tf_op | source)
XLA Modules:
  0.0 207.8 jit_solution(5729770105521794306)
XLA Ops:
  0.6 134.4 %coupled_step.1 = (bf16[48,64,256]{2,1,0:T(8,128)(2,1)}, bf16[24,128,128]{2,1,0:T(8,128)(2,1)}) custom-call(bf16[48,64,256]{2,1,0:T(8,128)(2,1)} %atm.1, bf16[24,128,128]{2,1,0:T(8,128)(2,1)} %water.1, s32[24,128]{1,0:T(8,128)} %mask_h.1, s32[24,4,128]{2,1,0:T(4,128)} %bitcast.8, f32[24,4,128]{2,1,0:T(4,128)} %bitcast.9, s32[48,4,64]{2,1,0:T(4,128)} %bitcast.6, ...), custom_call_target="tpu_custom_call" | custom-call | flops 8999999488 | bytes 20000000 | tf_op jit(solution)/shard_map/coupled_step/pallas_call | solution.py:780
  135.1 72.7 %settle.1 = (bf16[48,64,256]{2,1,0:T(8,128)(2,1)}, bf16[24,128,128]{2,1,0:T(8,128)(2,1)}) custom-call(bf16[48,64,256]{2,1,0:T(8,128)(2,1)} %get-tuple-element.4.refs_0_, bf16[24,128,128]{2,1,0:T(8,128)(2,1)} %get-tuple-element.5.refs_1_), custom_call_target="tpu_custom_call" | custom-call | tf_op jit(solution)/shard_map/settle/pallas_call | solution.py:754

commit v3 on v2

--- a/solution.py
+++ b/solution.py
@@ -390,23 +390,37 @@
         lax.fori_loop(0, 4, analyse_fields, 0)
         pl.semaphore_wait(ready, NR - 1)
 
-        for t in range(LT):
-            def force(b, _, t=t):
+        HALVES = ((1, ND // 2), (ND // 2, ND))
+
+        def scatter(t, h):
+            if h == 0:
+                pltpu.make_async_copy(sp.at[t, flat], rx.at[t, flat], r2.at[t]).start()
+
+            def step(p, _):
+                r_to, c_to = partner(p)
+                send(sp.at[t, r_to * NC + c_to], rx.at[t, flat], s2s.at[t, h], r2.at[t], (me, r_to, c_to))
+                return 0
+
+            lax.fori_loop(*HALVES[h], step, 0)
+
+        def scattered(t, h):
+            drain(sp.at[t, 0 : HALVES[h][1] - HALVES[h][0]], s2s.at[t, h])
+
+        def force(t):
+            def step(b, _):
                 rows = pl.ds(pl.multiple_of(b * FB, FB), FB)
                 got = ya[t, rows, :] + dot(us[rows, :], drv3[t])
                 halves = [got[:, h * 128 : (h + 1) * 128].reshape(FB // 8, 8, 128) for h in range(2)]
                 sp[t, pl.ds(b * (FB // 8), FB // 8)] = jnp.concatenate(halves, axis=1).astype(BF16)
                 return 0
 
-            lax.fori_loop(0, 4, force, 0)
-            pltpu.make_async_copy(sp.at[t, flat], rx.at[t, flat], r2.at[t]).start()
-
-            def scatter(p, _, t=t):
-                r_to, c_to = partner(p)
-                send(sp.at[t, r_to * NC + c_to], rx.at[t, flat], s2s.at[t], r2.at[t], (me, r_to, c_to))
-                return 0
-
-            lax.fori_loop(1, ND, scatter, 0)
+            lax.fori_loop(0, 4, step, 0)
+
+        force(0)
+        scatter(0, 0)
+        scatter(0, 1)
+        for t in range(1, LT):
+            force(t)
 
         drain(ss.at[0:HC], shr)
 
@@ -419,6 +433,9 @@
 
         lax.fori_loop(0, NC, lift_here, 0)
 
+        scattered(0, 0)
+        scatter(1, 0)
+
         drain(fb, ld.at[3])
         lat_in = lax.broadcasted_iota(jnp.int32, (NLAT, NLAT), 0)
         lat_to = lax.broadcasted_iota(jnp.int32, (NLAT, NLAT), 1)
@@ -430,6 +447,27 @@
             return 0
 
         lax.fori_loop(0, KB, reorder, 0)
+        scattered(0, 1)
+        scatter(1, 1)
+
+        halo_recv(tf, ef, efl, efr, PT, 8)
+        halo_sent(tf, ef, efl, efr, PT, 8, 0, 2)
+        tf[...] = (tf[...].astype(F32) + halo_columns(efl, efr, PT, PM)).astype(BF16)
+
+        for n, ref in ((15, mask), (16, oidx), (17, ow), (18, flw)):
+            drain(ref, ld.at[n])
+
+        def to_ocean(j, _):
+            i = me * HO + j
+            idx = jnp.concatenate([oidx[2 * i], oidx[2 * i + 1]], axis=1)
+            wgt = jnp.concatenate([ow[2 * i], ow[2 * i + 1]], axis=1)
+            fx[i] = regrid(tf, idx, wgt, AR, AC, 10 if AR % 10 == 0 else 1).astype(BF16)
+            send(fx.at[i], fx.at[i], fxs, fxr, (other, row, col))
+            return 0
+
+        lax.fori_loop(0, HO, to_ocean, 0)
+        scattered(1, 0)
+        scatter(2, 0)
 
         for q in range(2):
             for n, (there, dst) in enumerate(water_recvs(q)):
@@ -499,22 +537,8 @@
         lax.fori_loop(0, HR_ // 2, conv_first, 0)
         send(hd.at[me], hd.at[me], hds, hdr, (other, row, col))
 
-        halo_recv(tf, ef, efl, efr, PT, 8)
-        halo_sent(tf, ef, efl, efr, PT, 8, 0, 2)
-        tf[...] = (tf[...].astype(F32) + halo_columns(efl, efr, PT, PM)).astype(BF16)
-
-        for n, ref in ((15, mask), (16, oidx), (17, ow), (18, flw)):
-            drain(ref, ld.at[n])
-
-        def to_ocean(j, _):
-            i = me * HO + j
-            idx = jnp.concatenate([oidx[2 * i], oidx[2 * i + 1]], axis=1)
-            wgt = jnp.concatenate([ow[2 * i], ow[2 * i + 1]], axis=1)
-            fx[i] = regrid(tf, idx, wgt, AR, AC, 10 if AR % 10 == 0 else 1).astype(BF16)
-            send(fx.at[i], fx.at[i], fxs, fxr, (other, row, col))
-            return 0
-
-        lax.fori_loop(0, HO, to_ocean, 0)
+        scattered(1, 1)
+        scatter(2, 1)
 
         TB = 32 if ND % 32 == 0 else 8
 
@@ -570,8 +594,22 @@
 
         lax.fori_loop(0, KB, mix, 0)
 
-        for t in range(LT):
-            def to_synth(k, _, t=t):
+        def gather_back(t, h):
+            if h == 0:
+                pltpu.make_async_copy(qb.at[t, flat], vx.at[t, flat], q_r.at[t]).start()
+
+            def step(p, _):
+                r_to, c_to = partner(p)
+                send(qb.at[t, r_to * NC + c_to], vx.at[t, flat], q_s.at[t, h], q_r.at[t], (me, r_to, c_to))
+                return 0
+
+            lax.fori_loop(*HALVES[h], step, 0)
+
+        def gathered(t, h):
+            drain(vx.at[t, 0 : HALVES[h][1] - HALVES[h][0]], q_s.at[t, h])
+
+        def synth(t):
+            def to_synth(k, _):
                 basis = ib[k].reshape(NR, LT, NC, DEG)[:, t].reshape(ND, DEG)
                 got = dot(basis, ms[k])
                 for h in range(2):
@@ -580,21 +618,23 @@
 
             lax.fori_loop(0, KB, to_synth, 0)
 
-            def narrow(i, _, t=t):
+            def narrow(i, _):
                 rows = pl.ds(pl.multiple_of(i * TB, TB), TB)
                 in_rows = pl.ds(pl.multiple_of(i * TB * 16, TB * 16), TB * 16)
                 qb[t, rows] = qf[in_rows, :].reshape(TB, 16, 128).astype(BF16)
                 return 0
 
             lax.fori_loop(0, ND // TB, narrow, 0)
-            pltpu.make_async_copy(qb.at[t, flat], vx.at[t, flat], q_r.at[t]).start()
-
-            def gather_back(p, _, t=t):
-                r_to, c_to = partner(p)
-                send(qb.at[t, r_to * NC + c_to], vx.at[t, flat], q_s.at[t], q_r.at[t], (me, r_to, c_to))
-                return 0
-
-            lax.fori_loop(1, ND, gather_back, 0)
+
+        synth(0)
+        gather_back(0, 0)
+        gather_back(0, 1)
+        synth(1)
+        gathered(0, 0)
+        gather_back(1, 0)
+        synth(2)
+        gathered(0, 1)
+        gather_back(1, 1)
 
         drain(hd.at[0], hdr)
         drain(fx.at[0:HO], fxr)
@@ -614,15 +654,17 @@
 
         lax.fori_loop(0, WY // 2, conv_second, 0)
         pltpu.make_async_copy(oo, ocean_out, outs.at[0]).start()
+        gathered(1, 0)
+        gather_back(2, 0)
 
         drain(tab, ld.at[7])
-        for t in range(LT):
+        def to_grid(t):
             drain(vx.at[t], q_r.at[t])
             for h in range(2):
                 part = vx[t].astype(F32)[:, 8 * h : 8 * h + 8, :].reshape(NLON, 128)
                 bx[:, h * 128 : (h + 1) * 128] = part.astype(BF16)
 
-            def synthesise(b, _, t=t):
+            def synthesise(b, _):
                 y = lax.rem(col // NX + b, NY)
                 rows = pl.ds(pl.multiple_of(y * NX * PM, NX * PM), NX * PM)
                 gs[t, rows, :] = dot(tab[rows, :], bx[...]).astype(BF16)
@@ -648,10 +690,10 @@
 
             lax.fori_loop(0, NY, synthesise, 0)
 
-        for t in range(LT):
+        def finish_lats(t):
             drain(hh.at[t * NC : (t + 1) * NC], gsr.at[t])
 
-            def finish(c, _, t=t):
+            def finish(c, _):
                 n = t * NC + c
                 lf[n] = (lf[n].astype(F32) + gelu(hh[n].astype(F32))).astype(BF16)
                 return 0
@@ -660,11 +702,21 @@
             done = pl.ds(t * NC, NC)
             pltpu.make_async_copy(lf.at[done], atm_out.at[done], outs.at[1]).start()
 
+        to_grid(0)
+        gathered(1, 1)
+        gather_back(2, 1)
+        to_grid(1)
+        finish_lats(0)
+        to_grid(2)
+        finish_lats(1)
+        finish_lats(2)
+
         for t in range(LT):
             drain(g1.at[t, 0 : (NC - 1) * PM], g1s.at[t])
-            drain(sp.at[t, 0 : ND - 1], s2s.at[t])
-            drain(vx.at[t, 0 : ND - 1], q_s.at[t])
             drain(gs.at[t, 0 : (NC - 1) * PM], gss.at[t])
+        for h in range(2):
+            scattered(LT - 1, h)
+            gathered(LT - 1, h)
         drain(sr.at[0 : NC - 1], sss)
 
         @pl.when((col < me * HC) | (col >= me * HC + HC))
@@ -710,8 +762,8 @@
         v((4, LANES), F32), v((4, LANES), F32), v((4, LANES), F32),
         v((NC, NF, LANES), BF16), v((NC, NF, LANES), BF16), v((WY // 2, NF, LANES), BF16),
         dma((19,)), dma((9, 2)), dma((9, 2)), dma((2,)), dma((2,)), dma((16,)), dma((16,)),
-        dma((LT,)), dma((LT,)), dma, dma, dma((LT,)), dma((LT,)), dma((KB,)), dma((KB,)),
-        dma((LT,)), dma((LT,)), dma((LT,)), dma((LT,)), dma, dma, dma((2,)), dma, dma, dma, dma, pltpu.SemaphoreType.REGULAR,
+        dma((LT,)), dma((LT,)), dma, dma, dma((LT, 2)), dma((LT,)), dma((KB,)), dma((KB,)),
+        dma((LT, 2)), dma((LT,)), dma((LT,)), dma((LT,)), dma, dma, dma((2,)), dma, dma, dma, dma, pltpu.SemaphoreType.REGULAR,
     ]
     any_ = pl.BlockSpec(memory_space=pl.ANY)
     return pl.pallas_call(
@@ -732,31 +784,23 @@
 
 
 def settle(*arrays):
-    pieces = 8 if all(a.shape[0] % 8 == 0 for a in arrays) else 4
+    pieces = 4
+    count = len(arrays)
 
     def kernel(*refs):
-        count = len(arrays)
-        sems = refs[-1]
-        copies = []
         for n in range(count):
-            step = arrays[n].shape[0] // pieces
-            for p in range(pieces):
-                part = pl.ds(p * step, step)
-                copies.append(
-                    pltpu.make_async_copy(refs[n].at[part], refs[count + n].at[part], sems.at[n, p])
-                )
-        for copy in copies:
-            copy.start()
-        for copy in copies:
-            copy.wait()
-
-    any_ = pl.BlockSpec(memory_space=pl.ANY)
+            refs[count + n][...] = refs[n][...]
+
+    specs = [
+        pl.BlockSpec((a.shape[0] // pieces,) + a.shape[1:], lambda i: (i, 0, 0)) for a in arrays
+    ]
     return pl.pallas_call(
         kernel,
         out_shape=tuple(jax.ShapeDtypeStruct(a.shape, a.dtype) for a in arrays),
-        in_specs=[any_] * len(arrays),
-        out_specs=tuple([any_] * len(arrays)),
-        scratch_shapes=[pltpu.SemaphoreType.DMA((len(arrays), pieces))],
+        grid=(pieces,),
+        in_specs=specs,
+        out_specs=tuple(specs),
+        compiler_params=pltpu.CompilerParams(vmem_limit_bytes=32 * 1024 * 1024),
         name="settle",
     )(*arrays)
 

time: 208 us -> 141 us (0.68)
  Pallas kernels: 207 us -> 137 us
  local copies, waits for them, and re-layouts: 0 us -> 2.53 us
    pallas_call x1, Pallas kernels: 72.7 us -> 1.88 us  [settle(): pl.pallas_call(kernel, out_shape=tuple((jax.ShapeDtypeStruct(a.shape, a.d...]
    unnamed x0 -> x4, local copies, waits for them, and re-layouts: none -> 2.53 us
where the time goes in v3:
time: 141 us; the launch traced here: 140 us
  Pallas kernels  137 us (97%)
  local copies, waits for them, and re-layouts  2.53 us (2%)
    pallas_call x1, Pallas kernels, local(): step(atmosphere_state, water_condition, ocean_cell_mask, jnp.swapaxes(atm...  135 us

profile of v3, /device:TPU:8, one launch (start us, length us, event | category | flops | bytes accessed | tf_op | source)
XLA Modules:
  0.0 140.4 jit_solution(7030678257030469207)
XLA Ops:
  0.6 135.3 %coupled_step.1 = (bf16[48,64,256]{2,1,0:T(8,128)(2,1)}, bf16[24,128,128]{2,1,0:T(8,128)(2,1)}) custom-call(bf16[48,64,256]{2,1,0:T(8,128)(2,1)} %atm.1, bf16[24,128,128]{2,1,0:T(8,128)(2,1)} %water.1, s32[24,128]{1,0:T(8,128)} %mask_h.1, s32[24,4,128]{2,1,0:T(4,128)} %bitcast.8, f32[24,4,128]{2,1,0:T(4,128)} %bitcast.9, s32[48,4,64]{2,1,0:T(4,128)} %bitcast.6, ...), custom_call_target="tpu_custom_call" | custom-call | flops 8999999488 | bytes 20000000 | tf_op jit(solution)/shard_map/coupled_step/pallas_call | solution.py:824
  135.9 0.0 copy-start
  135.9 1.4 copy-done
  137.3 0.0 copy-start.1
  137.3 1.1 copy-done.1
  138.5 1.9 %settle.1 = (bf16[48,64,256]{2,1,0:T(8,128)(2,1)}, bf16[24,128,128]{2,1,0:T(8,128)(2,1)}) custom-call(bf16[48,64,256]{2,1,0:T(8,128)(2,1)S(1)} %copy-done, bf16[24,128,128]{2,1,0:T(8,128)(2,1)S(1)} %copy-done.1), custom_call_target="tpu_custom_call" | custom-call | tf_op jit(solution)/shard_map/settle/pallas_call | solution.py:797
Async XLA Ops:
  135.9 1.4 %copy-start = (bf16[48,64,256]{2,1,0:T(8,128)(2,1)S(1)}, bf16[48,64,256]{2,1,0:T(8,128)(2,1)}, u32[]{:S(2)}) copy-start(bf16[48,64,256]{2,1,0:T(8,128)(2,1)} %get-tuple-element.4.refs_0_) | copy-start | bytes 4718596
  137.3 1.1 copy-start.1

commit v4 on v3

--- a/solution.py
+++ b/solution.py
@@ -87,8 +87,20 @@
             xx = lax.rem(lax.rem(col, NX) + px, NX)
             return y * NX + xx
 
-        def partner(p):
-            return rmod(row + lax.rem(p, NR)), shifted(p // (NR * NX), lax.rem(p // NR, NX))
+        def all_partners(half, start):
+            def line_of(c_to, first):
+                for d in range(first, NR):
+                    r_to = row + d
+                    start(jnp.where(r_to >= NR, r_to - NR, r_to), c_to)
+
+            if half == 0:
+                line_of(col, 1)
+
+            def step(p, _):
+                line_of(shifted(p // NX, lax.rem(p, NX)), 0)
+                return 0
+
+            lax.fori_loop(1 if half == 0 else NC // 2, NC // 2 if half == 0 else NC, step, 0)
 
         def send(src, dst, ssem, rsem, dev):
             pltpu.make_async_remote_copy(
@@ -204,8 +216,6 @@
                 ((row > 0) & (col > 0), hl.at[q, W8]),
             ]
 
-        send_lat(0)
-
         def water_send(first, last):
             for q in range(2):
                 for n, (there, src, dst, dev) in enumerate(water_sends(q)[first:last]):
@@ -213,7 +223,6 @@
                     def _(src=src, dst=dst, dev=dev, n=n, q=q):
                         send(src, dst, wsend.at[first + n, q], wrecv.at[first + n, me], dev)
 
-        water_send(0, 2)
 
         def both(part):
             return (part[0].astype(F32) + part[1].astype(F32)).astype(BF16)
@@ -307,23 +316,9 @@
         ts[0 : WY * NF, 0:128] = both(ps)
         halo_send(ts, es, esl, esr, WY, WX, 0)
 
-        drain(atm_v, ld.at[0])
-        drain(fwt, ld.at[11])
-
-        def project_air(t, _):
-            cells = atm_v[pl.ds(t * 4, 4)].reshape(4 * PM, C)
-            got = dot_nt(fwt[...], cells)
-            zeros = jnp.zeros((NF, 128 - PM), F32)
-            for j in range(4):
-                part = jnp.concatenate([got[:, j * PM : (j + 1) * PM], zeros], axis=1)
-                pf[me, pl.ds((t * 4 + j) * NF, NF), :] = part.astype(BF16)
-            return 0
-
-        lax.fori_loop(0, PT // 4, project_air, 0)
-        send(pf.at[me], pf.at[me], csend.at[1], crecv.at[1], (other, row, col))
-
+        send_lat(0)
+        halo_recv(ts, es, esl, esr, WY, 0)
         send_lat(1)
-        halo_recv(ts, es, esl, esr, WY, 0)
         halo_sent(ts, es, esl, esr, WY, 0, 0, 2)
         ts[:, 128:256] = halo_columns(esl, esr, WY, 0).astype(BF16)
 
@@ -354,24 +349,22 @@
 
         lax.fori_loop(0, HC, to_air, 0)
         send_lat(2)
-        lax.fori_loop(0, W8, pack_edges, 0)
-        water_send(2, 8)
-        send(water, x.at[me, 2 : 2 + WY, 0:WX], wsend.at[8, 0], wrecv.at[8, 0], (other, row, col))
-        drain(pf.at[0], crecv.at[1])
-        tf[0 : PT * NF, :] = both(pf)
-        halo_send(tf, ef, efl, efr, PT, PM, 8)
-
         drain(tabt, ld.at[2])
 
-        for t in range(LT):
+        def analyse(t):
             drain(g1.at[t], g1r.at[t])
 
-            def analyse(b, _, t=t):
+            def step(b, _):
                 rows = pl.ds(pl.multiple_of(b * FB, FB), FB)
                 ya[t, rows, :] = dot(tabt[rows, :], g1[t])
                 return 0
 
-            lax.fori_loop(0, 4, analyse, 0)
+            lax.fori_loop(0, 4, step, 0)
+
+        analyse(0)
+        lax.fori_loop(0, W8, pack_edges, 0)
+        water_send(0, 8)
+        send(water, x.at[me, 2 : 2 + WY, 0:WX], wsend.at[8, 0], wrecv.at[8, 0], (other, row, col))
 
         drv3[...] = jnp.zeros(drv3.shape, BF16)
         for t in range(LT):
@@ -396,12 +389,10 @@
             if h == 0:
                 pltpu.make_async_copy(sp.at[t, flat], rx.at[t, flat], r2.at[t]).start()
 
-            def step(p, _):
-                r_to, c_to = partner(p)
+            def start(r_to, c_to):
                 send(sp.at[t, r_to * NC + c_to], rx.at[t, flat], s2s.at[t, h], r2.at[t], (me, r_to, c_to))
-                return 0
-
-            lax.fori_loop(*HALVES[h], step, 0)
+
+            all_partners(h, start)
 
         def scattered(t, h):
             drain(sp.at[t, 0 : HALVES[h][1] - HALVES[h][0]], s2s.at[t, h])
@@ -419,8 +410,31 @@
         force(0)
         scatter(0, 0)
         scatter(0, 1)
-        for t in range(1, LT):
-            force(t)
+
+        drain(atm_v, ld.at[0])
+        drain(fwt, ld.at[11])
+
+        def project_air(t, _):
+            cells = atm_v[pl.ds(t * 4, 4)].reshape(4 * PM, C)
+            got = dot_nt(fwt[...], cells)
+            zeros = jnp.zeros((NF, 128 - PM), F32)
+            for j in range(4):
+                part = jnp.concatenate([got[:, j * PM : (j + 1) * PM], zeros], axis=1)
+                pf[me, pl.ds((t * 4 + j) * NF, NF), :] = part.astype(BF16)
+            return 0
+
+        lax.fori_loop(0, PT // 4, project_air, 0)
+        send(pf.at[me], pf.at[me], csend.at[1], crecv.at[1], (other, row, col))
+
+        analyse(1)
+        force(1)
+        scattered(0, 0)
+        scatter(1, 0)
+        analyse(2)
+        force(2)
+        drain(pf.at[0], crecv.at[1])
+        tf[0 : PT * NF, :] = both(pf)
+        halo_send(tf, ef, efl, efr, PT, PM, 8)
 
         drain(ss.at[0:HC], shr)
 
@@ -433,8 +447,8 @@
 
         lax.fori_loop(0, NC, lift_here, 0)
 
-        scattered(0, 0)
-        scatter(1, 0)
+        scattered(0, 1)
+        scatter(1, 1)
 
         drain(fb, ld.at[3])
         lat_in = lax.broadcasted_iota(jnp.int32, (NLAT, NLAT), 0)
@@ -447,8 +461,6 @@
             return 0
 
         lax.fori_loop(0, KB, reorder, 0)
-        scattered(0, 1)
-        scatter(1, 1)
 
         halo_recv(tf, ef, efl, efr, PT, 8)
         halo_sent(tf, ef, efl, efr, PT, 8, 0, 2)
@@ -598,12 +610,10 @@
             if h == 0:
                 pltpu.make_async_copy(qb.at[t, flat], vx.at[t, flat], q_r.at[t]).start()
 
-            def step(p, _):
-                r_to, c_to = partner(p)
+            def start(r_to, c_to):
                 send(qb.at[t, r_to * NC + c_to], vx.at[t, flat], q_s.at[t, h], q_r.at[t], (me, r_to, c_to))
-                return 0
-
-            lax.fori_loop(*HALVES[h], step, 0)
+
+            all_partners(h, start)
 
         def gathered(t, h):
             drain(vx.at[t, 0 : HALVES[h][1] - HALVES[h][0]], q_s.at[t, h])
@@ -783,28 +793,6 @@
     )
 
 
-def settle(*arrays):
-    pieces = 4
-    count = len(arrays)
-
-    def kernel(*refs):
-        for n in range(count):
-            refs[count + n][...] = refs[n][...]
-
-    specs = [
-        pl.BlockSpec((a.shape[0] // pieces,) + a.shape[1:], lambda i: (i, 0, 0)) for a in arrays
-    ]
-    return pl.pallas_call(
-        kernel,
-        out_shape=tuple(jax.ShapeDtypeStruct(a.shape, a.dtype) for a in arrays),
-        grid=(pieces,),
-        in_specs=specs,
-        out_specs=tuple(specs),
-        compiler_params=pltpu.CompilerParams(vmem_limit_bytes=32 * 1024 * 1024),
-        name="settle",
-    )(*arrays)
-
-
 def solution(mesh):
     NR, NC = mesh.shape["row"], mesh.shape["col"]
     NX = 4 if NC == 16 else NC
@@ -821,7 +809,7 @@
         step = make_kernel(
             NR, NC, NX, PT, PM, C, WY, WX, CO, flux_weight.shape[1], forward_basis.shape[1]
         )
-        return settle(*step(
+        return step(
             atmosphere_state,
             water_condition,
             ocean_cell_mask,
@@ -841,7 +829,7 @@
             second_ocean_kernel,
             jnp.asarray(table),
             jnp.asarray(np.ascontiguousarray(table.T)),
-        ))
+        )
 
     placed = (
         P("row", "col", "comp"),

time: 141 us -> 137 us (0.972)
  Pallas kernels: 137 us -> 132 us
    pallas_call x1, Pallas kernels: 135 us -> 132 us  [local(): step(atmosphere_state, water_condition, ocean_cell_mask, jnp.swapaxes(atm...]
    pallas_call x1 -> x0, Pallas kernels: 1.88 us -> none  [settle(): pl.pallas_call(kernel, out_shape=tuple((jax.ShapeDtypeStruct(a.shape, a.d...]
where the time goes in v4:
time: 137 us; the launch traced here: 136 us
  Pallas kernels  132 us (96%)
  local copies, waits for them, and re-layouts  3.68 us (3%)
    pallas_call x1, Pallas kernels, local(): step(atmosphere_state, water_condition, ocean_cell_mask, jnp.swapaxes(atm...  132 us
    unnamed x4, local copies, waits for them, and re-layouts  3.68 us

profile of v4, /device:TPU:8, one launch (start us, length us, event | category | flops | bytes accessed | tf_op | source)
XLA Modules:
  0.0 136.5 jit_solution(14984942037801782447)
XLA Ops:
  0.6 132.2 %coupled_step.1 = (bf16[48,64,256]{2,1,0:T(8,128)(2,1)}, bf16[24,128,128]{2,1,0:T(8,128)(2,1)}) custom-call(bf16[48,64,256]{2,1,0:T(8,128)(2,1)} %atm.1, bf16[24,128,128]{2,1,0:T(8,128)(2,1)} %water.1, s32[24,128]{1,0:T(8,128)} %mask_h.1, s32[24,4,128]{2,1,0:T(4,128)} %bitcast.8, f32[24,4,128]{2,1,0:T(4,128)} %bitcast.9, s32[48,4,64]{2,1,0:T(4,128)} %bitcast.6, ...), custom_call_target="tpu_custom_call" | custom-call | flops 8999999488 | bytes 20000000 | tf_op jit(solution)/shard_map/coupled_step/pallas_call | solution.py:812
  132.8 0.0 copy-start
  132.8 2.8 %copy.23 = bf16[48,64,256]{2,1,0:T(8,128)(2,1)} copy(bf16[48,64,256]{2,1,0:T(8,128)(2,1)} %get-tuple-element.4) | data formatting | bytes 3145728
  135.6 0.0 copy-done
  135.6 0.9 copy.24
Async XLA Ops:
  132.8 2.8 %copy-start = (bf16[24,128,128]{2,1,0:T(8,128)(2,1)S(1)}, bf16[24,128,128]{2,1,0:T(8,128)(2,1)}, u32[]{:S(2)}) copy-start(bf16[24,128,128]{2,1,0:T(8,128)(2,1)} %get-tuple-element.5) | copy-start | bytes 2359300
